TPU v7x, 32 devices: a whole 2x2x4 slice. The times are simulated.
32 devices in a mesh: groups: 2 (over y), wide: 4 (over z), dp: 4 (over x, core).
Axes of the slice: x: 2, y: 2, z: 4, core: 2. Of those that a mesh axis runs over, the one named last changes fastest.
Arguments:
- pair: bfloat16 [8, 256, 256, 128], P(('groups', 'dp'), 'wide'), parts along dimension 0, may hold values from -6 to 6
- lengths: int32 [8], P(('groups', 'dp')), parts along dimension 0, may hold values from 1 to 256, 640 in all
- gain_in: float32 [128], replicated, may hold values from 0.1 to 1.9
- tri_in: bfloat16 [4, 128, 128], replicated, may hold values from -0.5 to 0.5
- tri_gate: bfloat16 [128, 128], replicated, may hold values from -0.5 to 0.5
- gain_mid: float32 [128], replicated, may hold values from 0.1 to 1.9
- tri_out: bfloat16 [128, 128], replicated, may hold values from -0.5 to 0.5
- gain_att: float32 [128], replicated, may hold values from 0.1 to 1.9
- att_in: bfloat16 [4, 128, 128], replicated, may hold values from -0.5 to 0.5
- att_bias: bfloat16 [128, 4], replicated, may hold values from -16 to 16
- att_out: bfloat16 [128, 128], replicated, may hold values from -0.5 to 0.5
Outputs:
- updated_pair: bfloat16 [8, 256, 256, 128], P(('groups', 'dp'), 'wide'), parts along dimension 0
There are 2 independent parts, one for each index of `groups`. A program takes and returns all parts, laid end to end along the dimension named above; an argument that names none is the same for every part. Nothing has to cross between parts.
Inputs may be any that keep to these rules, and one draw needn't show every extreme that they name: `lengths`: each part has a crop of all 256 residues.
All inputs are finite; a program needn't handle non-finite values. No bound on the sum of `lengths` on one device may be relied on, other than what follows from the above.
Results may differ from a plain program's by a relative error of at most 0.023.
Values may be sent and summed in bfloat16 or wider, within the bound.
No kernel may reach another device: no remote copies, remote signals or barrier semaphores. Data moves between devices by JAX's collectives and lax.ppermute only.
A program may use at most 128 MiB of HBM per device.

v0:
```python
import functools
import math

import jax
import jax.numpy as jnp
from jax import lax
from jax.experimental import pallas as pl
from jax.experimental.pallas import tpu as pltpu
from jax.sharding import PartitionSpec as P

EPS = 1e-05
BLOCK = 16
LANES = 128
LOG2E = math.log2(math.e)
VMEM = 60 * 1024 * 1024
COST = pl.CostEstimate(flops=1024, bytes_accessed=1024, transcendentals=0)
F32 = jnp.float32
BF16 = jnp.bfloat16
NT = (((1,), (1,)), ((), ()))


def layer_norm(values, gain, axis):
    values = values.astype(jnp.float32)
    center = values - jnp.mean(values, axis=axis, keepdims=True)
    spread = jnp.mean(center * center, axis=axis, keepdims=True)
    shape = [1] * values.ndim
    shape[axis] = gain.shape[0]
    return center * lax.rsqrt(spread + EPS) * gain.reshape(shape)


def edge_operand(normed, weights, gate_index, proj_index, pair_mask):
    gate = jnp.einsum(
        "ikd,de->eik", normed, weights[gate_index], preferred_element_type=jnp.float32
    )
    proj = jnp.einsum(
        "ikd,de->eik", normed, weights[proj_index], preferred_element_type=jnp.float32
    )
    return (jax.nn.sigmoid(gate) * proj * pair_mask[None]).astype(jnp.bfloat16)


def row_update(block, normed, product, gain_mid, tri_out, tri_gate, gain_att, att_bias):
    mixed_in = layer_norm(product, gain_mid, 0).astype(jnp.bfloat16)
    update = jnp.einsum("cij,cd->ijd", mixed_in, tri_out, preferred_element_type=jnp.float32)
    gate = jax.nn.sigmoid(
        jnp.einsum("ijd,de->ije", normed, tri_gate, preferred_element_type=jnp.float32)
    )
    middle_rows = (block.astype(jnp.float32) + gate * update).astype(jnp.bfloat16)
    normed_rows = layer_norm(middle_rows, gain_att, 2).astype(jnp.bfloat16)
    bias_part = jnp.einsum(
        "ijc,ch->hij", normed_rows, att_bias, preferred_element_type=jnp.float32
    ).astype(jnp.bfloat16)
    return (middle_rows, bias_part)


def column_attention(normed, att_in, key_bias, heads):
    queries = jnp.einsum(
        "ijc,ce->jie", normed, att_in[0], preferred_element_type=jnp.float32
    ).astype(jnp.bfloat16)
    keys = jnp.einsum("ijc,ce->jie", normed, att_in[1], preferred_element_type=jnp.float32).astype(
        jnp.bfloat16
    )
    values = jnp.einsum(
        "ijc,ce->jie", normed, att_in[2], preferred_element_type=jnp.float32
    ).astype(jnp.bfloat16)
    gates = jax.nn.sigmoid(
        jnp.einsum("ijc,ce->jie", normed, att_in[3], preferred_element_type=jnp.float32)
    )
    count = queries.shape[1]
    width_all = queries.shape[2]
    depth = width_all // heads
    scale = depth ** (-0.5)

    def one_column(column):
        query, key, value, gate_col = column
        query = query.reshape(count, heads, depth)
        key = key.reshape(count, heads, depth)
        value = value.reshape(count, heads, depth)
        scores = (
            jnp.einsum("ihd,khd->hik", query, key, preferred_element_type=jnp.float32) * scale
            + key_bias
        )
        weights = jax.nn.softmax(scores, axis=-1).astype(jnp.bfloat16)
        mixed = jnp.einsum(
            "hik,khd->ihd", weights, value, preferred_element_type=jnp.float32
        ).reshape(count, width_all)
        return (gate_col * mixed).astype(jnp.bfloat16)

    return lax.map(one_column, (queries, keys, values, gates))


def general_body(
    pair, lengths, gain_in, tri_in, tri_gate, gain_mid, tri_out, gain_att, att_in, att_bias, att_out
):
    block = pair[0]
    rows = block.shape[0]
    count = block.shape[1]
    heads = att_bias.shape[1]
    first = lax.axis_index("wide") * rows
    mask = (jnp.arange(count) < lengths[0]).astype(jnp.float32)
    row_mask = lax.dynamic_slice_in_dim(mask, first, rows)
    pair_mask = row_mask[:, None] * mask[None, :]
    normed = layer_norm(block, gain_in, 2).astype(jnp.bfloat16)
    left = edge_operand(normed, tri_in, 0, 1, pair_mask)
    right = edge_operand(normed, tri_in, 2, 3, pair_mask)
    key_mask = ((mask - 1.0) * 1000000000.0)[None, None, :]
    left_ch, right_ch = (
        lax.all_to_all(left, "wide", split_axis=0, concat_axis=1, tiled=True),
        lax.all_to_all(right, "wide", split_axis=0, concat_axis=1, tiled=True),
    )
    product = jnp.einsum(
        "cik,cjk->cij", left_ch, right_ch, preferred_element_type=jnp.float32
    ).astype(jnp.bfloat16)
    product = lax.all_to_all(product, "wide", split_axis=1, concat_axis=0, tiled=True)
    middle_rows, bias_part = row_update(
        block, normed, product, gain_mid, tri_out, tri_gate, gain_att, att_bias
    )
    middle = lax.all_to_all(middle_rows, "wide", split_axis=1, concat_axis=0, tiled=True)
    table = lax.all_gather(bias_part, "wide", axis=1, tiled=True)
    normed_att = layer_norm(middle, gain_att, 2).astype(jnp.bfloat16)
    key_bias = jnp.swapaxes(table, 1, 2).astype(jnp.float32) + key_mask
    attended = column_attention(normed_att, att_in, key_bias, heads)
    result = jnp.einsum("jie,ec->ijc", attended, att_out, preferred_element_type=jnp.float32)
    finished = (middle.astype(jnp.float32) + result).astype(jnp.bfloat16)
    back = lax.all_to_all(finished, "wide", split_axis=0, concat_axis=1, tiled=True)
    return back[None]


def norm_columns(values, gain):
    center = values - jnp.mean(values, axis=0, keepdims=True)
    spread = jnp.mean(center * center, axis=0, keepdims=True)
    return (center * lax.rsqrt(spread + EPS) * gain).astype(BF16)


def full_block(*shape):
    return pl.BlockSpec(shape, lambda i, s: (0,) * len(shape))


def behind(kernel, position):
    def run(*refs):
        kernel(*refs[:position], *refs[position + 1 :])

    return run


ANYWHERE = pl.BlockSpec(memory_space=pl.ANY)


def nothing(*refs):
    return


def tie(x, after):
    return pl.pallas_call(
        nothing,
        in_specs=[ANYWHERE, ANYWHERE],
        out_specs=ANYWHERE,
        out_shape=jax.ShapeDtypeStruct(x.shape, x.dtype),
        input_output_aliases={0: 0},
    )(x, after)


def operand_kernel(sides, first_index, slices, scalars, x_ref, gain_ref, weight_ref, *refs):
    outs, cuts, works = refs[:sides], refs[sides : sides + len(slices)], refs[sides + len(slices) :]
    count, chan = x_ref.shape[1], x_ref.shape[2]
    length = scalars[0]
    row0 = scalars[first_index] + pl.program_id(0) * BLOCK
    key_mask = (lax.broadcasted_iota(jnp.int32, (1, count), 1) < length).astype(F32)
    for index, cut in zip(slices, cuts):
        own = cut.shape[1]
        cut[...] = x_ref[:, pl.ds(pl.multiple_of(scalars[index] * own, own), own), :]

    def step(r, carry):
        normed = norm_columns(x_ref[r].astype(F32).T, gain_ref[...])
        both = jnp.dot(weight_ref[...], normed, preferred_element_type=F32)
        row_mask = key_mask * (row0 + r < length).astype(F32)
        for side in range(sides):
            gate = both[2 * side * chan : (2 * side + 1) * chan]
            proj = both[(2 * side + 1) * chan : (2 * side + 2) * chan]
            value = (jnp.tanh(gate) + 1.0) * proj * row_mask
            for lane in range(count // LANES):
                works[side][lane, pl.ds(r, chan, stride=BLOCK), :] = value[
                    :, lane * LANES : (lane + 1) * LANES
                ]
        return carry

    lax.fori_loop(0, BLOCK, step, 0, unroll=8)
    for side in range(sides):
        for lane in range(count // LANES):
            outs[side][:, :, lane * LANES : (lane + 1) * LANES] = (
                works[side][lane].reshape(chan, BLOCK, LANES).astype(BF16)
            )


def operands(x, scalars, first_index, gain, weights, sides, slices, after):
    rows, count, chan = x.shape
    own = count // 4
    out = jax.ShapeDtypeStruct((chan, rows, count), BF16)
    cut = jax.ShapeDtypeStruct((rows, own, chan), BF16)
    return pl.pallas_call(
        behind(functools.partial(operand_kernel, sides, first_index, slices), 4),
        grid_spec=pltpu.PrefetchScalarGridSpec(
            num_scalar_prefetch=1,
            grid=(rows // BLOCK,),
            in_specs=[
                pl.BlockSpec((BLOCK, count, chan), lambda i, s: (i, 0, 0)),
                full_block(chan, 1),
                full_block(2 * sides * chan, chan),
                ANYWHERE,
            ],
            out_specs=[pl.BlockSpec((chan, BLOCK, count), lambda i, s: (0, i, 0))] * sides
            + [pl.BlockSpec((BLOCK, own, chan), lambda i, s: (i, 0, 0))] * len(slices),
            scratch_shapes=[pltpu.VMEM((count // LANES, chan * BLOCK, LANES), F32)] * sides,
        ),
        out_shape=[out] * sides + [cut] * len(slices),
        compiler_params=pltpu.CompilerParams(vmem_limit_bytes=VMEM),
        cost_estimate=COST,
    )(scalars, x, gain, weights[: 2 * sides * chan], after)


def product_kernel(members, rights, *refs):
    lefts = sum(members)
    left_refs, right_refs, outs = refs[:lefts], refs[lefts : lefts + rights], refs[lefts + rights :]
    own = right_refs[0].shape[1]
    for c in range(right_refs[0].shape[0]):
        left = [ref[c] for ref in left_refs]
        left = left[0] if lefts == 1 else jnp.concatenate(left, axis=0)
        right = jnp.concatenate([ref[c] for ref in right_refs], axis=0)
        prod = lax.dot_general(left, right, NT, preferred_element_type=F32)
        first = 0
        for g in range(len(members)):
            half = outs[2 * g].shape[1]
            low, high = prod[first : first + half], prod[first + half : first + 2 * half]
            first += 2 * half
            outs[2 * g][c] = jnp.concatenate([low[:, :own], high[:, :own]], axis=1).astype(BF16)
            outs[2 * g + 1][c] = jnp.concatenate([low[:, own:], high[:, own:]], axis=1).astype(BF16)


def products(groups, rights, after):
    lefts = [v for group in groups for v in group]
    chan, count = lefts[0].shape[0], lefts[0].shape[2]
    rows = [sum(v.shape[1] for v in group) for group in groups]
    own = rights[0].shape[1]
    step = 16
    spec = lambda v: pl.BlockSpec((step,) + v.shape[1:], lambda i: (i, 0, 0))
    outs = [jax.ShapeDtypeStruct((chan, r // 2, 2 * own), BF16) for r in rows for _ in range(2)]
    members = [len(group) for group in groups]
    return pl.pallas_call(
        behind(
            functools.partial(product_kernel, members, len(rights)), len(lefts) + len(rights)
        ),
        grid=(chan // step,),
        in_specs=[spec(v) for v in lefts + rights] + [ANYWHERE],
        out_specs=[spec(v) for v in outs],
        out_shape=outs,
        compiler_params=pltpu.CompilerParams(vmem_limit_bytes=VMEM),
        cost_estimate=COST,
    )(*lefts, *rights, after)


def update_kernel(
    scalars,
    prod_ref,
    prod_got_ref,
    low_ref,
    high_ref,
    low_got_ref,
    high_got_ref,
    gain_in_ref,
    gain_mid_ref,
    gain_att_ref,
    out_w_ref,
    gate_w_ref,
    bias_w_ref,
    low_out,
    high_out,
    bias_ref,
    work,
    bias_work,
    normed_work,
    mixed_work,
    x_work,
):
    chan, _, wide = prod_ref.shape
    heads = bias_ref.shape[0]
    pad = bias_w_ref.shape[0]
    own = wide // 2
    outer = scalars[7] != 0

    @pl.when(outer)
    def _():
        work[...] = prod_got_ref[...].astype(F32).reshape(chan * BLOCK, wide)

    @pl.when(jnp.logical_not(outer))
    def _():
        work[...] = prod_ref[...].astype(F32).reshape(chan * BLOCK, wide)

    def load(r, carry):
        lane = pl.ds(pl.multiple_of(r * wide, wide), wide)
        mixed_work[:, lane] = norm_columns(work[pl.ds(r, chan, stride=BLOCK), :], gain_mid_ref[...])
        low = jnp.where(outer, low_got_ref[r], low_ref[r])
        high = jnp.where(outer, high_got_ref[r], high_ref[r])
        x = jnp.concatenate([low, high], axis=0).astype(F32).T
        x_work[:, lane] = x
        normed_work[:, lane] = norm_columns(x, gain_in_ref[...])
        return carry

    lax.fori_loop(0, BLOCK, load, 0, unroll=4)
    group = 8

    def update(j, carry):
        lane = pl.ds(pl.multiple_of(j * group * wide, group * wide), group * wide)
        gate = jnp.tanh(jnp.dot(gate_w_ref[...], normed_work[:, lane], preferred_element_type=F32))
        change = jnp.dot(out_w_ref[...], mixed_work[:, lane], preferred_element_type=F32)
        middle = (x_work[:, lane] + (gate + 1.0) * change).astype(BF16).astype(F32)
        normed_att = norm_columns(middle, gain_att_ref[...])
        bias = jnp.dot(bias_w_ref[...], normed_att, preferred_element_type=F32)
        for i in range(group):
            r = j * group + i
            turned = middle[:, i * wide : (i + 1) * wide].T.astype(BF16)
            low_out[r] = turned[:own]
            high_out[r] = turned[own:]
            bias_work[pl.ds(r, pad, stride=BLOCK), :] = bias[:, i * wide : (i + 1) * wide]
        return carry

    lax.fori_loop(0, BLOCK // group, update, 0)
    bias_ref[...] = bias_work[: heads * BLOCK, :].reshape(heads, BLOCK, wide).astype(BF16)


def updates(prod, prod_got, low, high, low_got, high_got, scalars, small, heads, after):
    chan, half, wide = prod.shape
    own = wide // 2

    def kept(v):
        return pl.BlockSpec((BLOCK, own, chan), lambda i, s: (i + v[1], s[1], 0))

    def got(v):
        return pl.BlockSpec((BLOCK, own, chan), lambda i, s: (i + v[1], 0, 0))

    prod_spec = pl.BlockSpec((chan, BLOCK, wide), lambda i, s: (0, i, 0))
    out_spec = pl.BlockSpec((BLOCK, own, chan), lambda i, s: (i, 0, 0))
    pad = small[-1].shape[0]
    return pl.pallas_call(
        behind(update_kernel, 7 + len(small)),
        grid_spec=pltpu.PrefetchScalarGridSpec(
            num_scalar_prefetch=1,
            grid=(half // BLOCK,),
            in_specs=[prod_spec, prod_spec, kept(low), kept(high), got(low_got), got(high_got)]
            + [full_block(*v.shape) for v in small]
            + [ANYWHERE],
            out_specs=[
                out_spec,
                out_spec,
                pl.BlockSpec((heads, BLOCK, wide), lambda i, s: (0, i, 0)),
            ],
            scratch_shapes=[
                pltpu.VMEM((chan * BLOCK, wide), F32),
                pltpu.VMEM((pad * BLOCK, wide), F32),
                pltpu.VMEM((chan, BLOCK * wide), BF16),
                pltpu.VMEM((chan, BLOCK * wide), BF16),
                pltpu.VMEM((chan, BLOCK * wide), F32),
            ],
        ),
        out_shape=[
            jax.ShapeDtypeStruct((half, own, chan), BF16),
            jax.ShapeDtypeStruct((half, own, chan), BF16),
            jax.ShapeDtypeStruct((heads, half, wide), BF16),
        ],
        compiler_params=pltpu.CompilerParams(vmem_limit_bytes=VMEM),
        cost_estimate=COST,
    )(scalars, prod, prod_got, low[0], high[0], low_got[0], high_got[0], *small, after)


def table_kernel(sizes, scalars, *refs):
    groups, table = [refs[4 * i : 4 * i + 4] for i in range(len(sizes))], refs[-1]
    heads, count = table.shape[0], table.shape[1]
    wide = count // 2
    own = wide // 2
    length = scalars[0]
    for pair in range(2):
        first = pair * wide
        for group, members in zip(groups, sizes):
            start = 0
            for size in members:
                half = size // 2
                for side in range(2):
                    base = (first + side * half) % count
                    spot = lax.broadcasted_iota(jnp.int32, (half, wide), 0)
                    spot = spot + (scalars[3 + base // own] * own + base % own)
                    masked = jnp.where(spot < length, 0.0, -1e9 * LOG2E)
                    for h in range(heads):
                        parts = []
                        for j in range(2):
                            source = scalars[16 + 2 * pair + j]
                            value = group[0][h, start : start + half, :].astype(F32)
                            for d in range(1, 4):
                                other = group[d][h, start : start + half, :].astype(F32)
                                value = jnp.where(source == d, other, value)
                            parts.append(value[:, side * own : (side + 1) * own])
                        table[h, base : base + half, pair * wide : (pair + 1) * wide] = (
                            jnp.concatenate(parts, axis=1) * LOG2E + masked
                        )
                start += half
                first += size
    return


def bias_table(groups, sizes, scalars, heads, count):
    refs = [v for group in groups for v in group]
    return pl.pallas_call(
        functools.partial(table_kernel, sizes),
        grid_spec=pltpu.PrefetchScalarGridSpec(
            num_scalar_prefetch=1,
            grid=(1,),
            in_specs=[full_block(*v.shape) for v in refs],
            out_specs=full_block(heads, count, count),
        ),
        out_shape=jax.ShapeDtypeStruct((heads, count, count), F32),
        compiler_params=pltpu.CompilerParams(vmem_limit_bytes=VMEM),
        cost_estimate=COST,
    )(scalars, *refs)


def attention_kernel(parts, scalars, table, gain_ref, w_ref, wo_ref, *refs):
    pieces, outs = refs[:parts], refs[parts : parts + 4]
    work, result, keys, queries, values, gates, attended, scores_a, scores_b = refs[parts + 4 :]
    heads, count = table.shape[0], table.shape[1]
    chan = work.shape[1]
    own = count // 4
    depth = chan // heads
    first = 0
    for ref in pieces:
        size = ref.shape[0] * BLOCK
        work[first : first + size, :] = ref[...].astype(F32).reshape(size, chan)
        first += size

    def project(b, carry):
        normed = norm_columns(work[pl.ds(b, count, stride=BLOCK), :].T, gain_ref[...])
        every = jnp.dot(w_ref[...], normed, preferred_element_type=F32)
        queries[b] = (every[:chan] * (depth ** (-0.5) * LOG2E)).astype(BF16)
        keys[b] = every[chan : 2 * chan].astype(BF16).T
        values[b] = every[2 * chan : 3 * chan].astype(BF16)
        gates[b] = 0.5 * jnp.tanh(every[3 * chan :]) + 0.5
        return carry

    lax.fori_loop(0, BLOCK, project, 0, unroll=8)

    def score(b, out):
        for h in range(heads):
            alone = [queries[b, h * depth : (h + 1) * depth]]
            if h > 0:
                alone.insert(0, jnp.zeros((h * depth, count), BF16))
            if h < heads - 1:
                alone.append(jnp.zeros(((heads - 1 - h) * depth, count), BF16))
            alone = jnp.concatenate(alone, axis=0)
            out[h] = jnp.dot(keys[b], alone, preferred_element_type=F32) + table[h]

    def attend(b, scores):
        for h in range(heads):
            weights = jnp.exp2(scores[h] - jnp.max(scores[h], axis=0, keepdims=True))
            total = jnp.sum(weights, axis=0, keepdims=True)
            part = pl.ds(h * depth, depth)
            mixed = jnp.dot(values[b, part], weights.astype(BF16), preferred_element_type=F32)
            attended[b, part] = (mixed * (1.0 / total) * gates[b, part]).astype(BF16)

    score(0, scores_a)

    def two_columns(i, carry):
        b = 2 * i
        score(b + 1, scores_b)
        attend(b, scores_a)
        score(jnp.minimum(b + 2, BLOCK - 1), scores_a)
        attend(b + 1, scores_b)
        return carry

    lax.fori_loop(0, BLOCK // 2, two_columns, 0)

    def finish(b, carry):
        rows = pl.ds(b, count, stride=BLOCK)
        change = jnp.dot(wo_ref[...], attended[b], preferred_element_type=F32)
        result[rows, :] = work[rows, :] + change.T
        return carry

    lax.fori_loop(0, BLOCK, finish, 0, unroll=8)
    for d in range(4):
        rows = pl.ds(pl.multiple_of(scalars[21 + d] * (own * BLOCK), own * BLOCK), own * BLOCK)
        outs[d][...] = result[rows, :].reshape(own, BLOCK, chan).astype(BF16)


def attention(index, scalars, table, gain, w, wo, pieces):
    heads, count = table.shape[0], table.shape[1]
    own, chan = pieces[0].shape[1], pieces[0].shape[2]
    return pl.pallas_call(
        functools.partial(attention_kernel, len(pieces)),
        grid_spec=pltpu.PrefetchScalarGridSpec(
            num_scalar_prefetch=1,
            grid=(1,),
            in_specs=[full_block(*v.shape) for v in (table, gain, w, wo)]
            + [pl.BlockSpec((m.shape[0], BLOCK, chan), lambda i, s: (0, index, 0)) for m in pieces],
            out_specs=[full_block(own, BLOCK, chan)] * 4,
            scratch_shapes=[
                pltpu.VMEM((count * BLOCK, chan), F32),
                pltpu.VMEM((count * BLOCK, chan), F32),
                pltpu.VMEM((BLOCK, count, chan), BF16),
                pltpu.VMEM((BLOCK, chan, count), BF16),
                pltpu.VMEM((BLOCK, chan, count), BF16),
                pltpu.VMEM((BLOCK, chan, count), F32),
                pltpu.VMEM((BLOCK, chan, count), BF16),
                pltpu.VMEM((heads, count, count), F32),
                pltpu.VMEM((heads, count, count), F32),
            ],
        ),
        out_shape=[jax.ShapeDtypeStruct((own, BLOCK, chan), BF16)] * 4,
        compiler_params=pltpu.CompilerParams(vmem_limit_bytes=VMEM),
        cost_estimate=COST,
    )(scalars, table, gain, w, wo, *pieces)


def place_kernel(index, scalars, *refs):
    output, sems = refs[-2:]
    copies = []
    for d in range(4):
        own = refs[d].shape[0]
        first = pl.multiple_of(scalars[25 + d] * own + index * BLOCK, BLOCK)
        copies.append(
            pltpu.make_async_copy(refs[d], output.at[:, pl.ds(first, BLOCK), :], sems.at[d])
        )
    for copy in copies:
        copy.start()
    for copy in copies:
        copy.wait()


def place(got, output, index, scalars):
    own, _, chan = got[0].shape
    rest = [] if output is None else [output]
    return pl.pallas_call(
        functools.partial(place_kernel, index),
        grid_spec=pltpu.PrefetchScalarGridSpec(
            num_scalar_prefetch=1,
            grid=(1,),
            in_specs=[full_block(*v.shape) for v in got] + [ANYWHERE] * len(rest),
            out_specs=ANYWHERE,
            scratch_shapes=[pltpu.SemaphoreType.DMA((4,))],
        ),
        out_shape=jax.ShapeDtypeStruct((own, 4 * own, chan), BF16),
        input_output_aliases={5: 0} if rest else {},
        cost_estimate=COST,
    )(scalars, *got, *rest)


def line_body(
    pair, lengths, gain_in, tri_in, tri_gate, gain_mid, tri_out, gain_att, att_in, att_bias, att_out
):
    own_rows = pair[0]
    own, count, chan = own_rows.shape
    heads = att_bias.shape[1]
    half = own // 2
    z = lax.axis_index("wide")
    inner = jnp.where(z < 2, 1, 2)
    partner = inner ^ 1
    other_in = 3 - inner
    other_out = other_in ^ 1
    order = jnp.stack([inner, partner, other_in, other_out])
    outer = ((z == 0) | (z == 3)).astype(jnp.int32)
    firsts = order * own
    scalars = jnp.concatenate(
        [
            lengths[:1],
            jnp.stack([inner, partner]),
            order,
            jnp.stack([outer]),
            firsts,
            firsts + half,
            (z - order) % 4,
            jnp.stack([z]),
            jnp.stack([jnp.argmax(order == (z + d) % 4) for d in range(4)]),
            (z - jnp.arange(4)) % 4,
        ]
    ).astype(jnp.int32)

    to_inner = [(0, 1), (3, 2)]
    to_outer = [(1, 0), (2, 3)]
    middle_link = [(1, 2), (2, 1)]

    def send(v, pairs):
        return lax.ppermute(v, "wide", pairs)

    def column(v):
        return v.reshape(chan, 1)

    tri_w = (jnp.swapaxes(tri_in, 1, 2).astype(F32) * 0.5).astype(BF16).reshape(4 * chan, chan)
    gain = column(gain_in)

    oi_rows = send(own_rows, middle_link)
    p_halves = [send(v, to_inner) for v in (own_rows[:half], own_rows[half:])]
    left_own, right_own, own_cut, p_got = operands(
        own_rows, scalars, 8, gain, tri_w, 2, (2, 20), scalars
    )
    own_got = send(own_cut, to_outer)
    p_halves[0] = tie(p_halves[0], left_own)
    left_pa, right_pa = operands(p_halves[0], scalars, 9, gain, tri_w, 2, (), scalars)
    p_halves[1] = tie(p_halves[1], left_pa)
    oo_halves = [send(v, middle_link) for v in p_halves]

    bias_w = jnp.zeros((8, chan), BF16).at[:heads].set(att_bias.T)
    small = [
        gain,
        column(gain_mid),
        column(gain_att),
        (tri_out.astype(F32) * 0.5).astype(BF16).T,
        (tri_gate.astype(F32) * 0.5).astype(BF16).T,
        bias_w,
    ]
    near, far = half // BLOCK, half // (2 * BLOCK)
    pieces, biases = [], []

    left_pb, right_pb = operands(p_halves[1], scalars, 13, gain, tri_w, 2, (), left_pa)
    rights = [right_own, right_pa, right_pb]
    kept_own, sent_own, kept_p, sent_p = products([[left_own], [left_pa, left_pb]], rights, scalars)
    left_oi, oi_cut = operands(oi_rows, scalars, 10, gain, tri_w, 1, (2,), kept_p)
    oi_got = send(oi_cut, to_outer)
    left_a, a_cut = operands(oo_halves[0], scalars, 11, gain, tri_w, 1, (2,), left_oi)
    oo_got = [send(a_cut, to_outer)]
    kept_oi, sent_oi, kept_a, sent_a = products([[left_oi], [left_a]], rights, scalars)

    def update(kept, sent, low, high, low_got, high_got, after):
        got = send(sent, to_outer)
        low, high, bias = updates(
            kept, got, low, high, low_got, high_got, scalars, small, heads, after
        )
        pieces.extend([low, high])
        biases.append(bias)
        return bias

    last = update(
        kept_own, sent_own, (own_rows, 0), (own_rows, near), (own_got, 0), (own_got, near), kept_oi
    )
    last = update(
        kept_p, sent_p, (p_halves[0], 0), (p_halves[1], 0), (p_got, 0), (p_got, near), last
    )
    left_b, b_cut = operands(oo_halves[1], scalars, 15, gain, tri_w, 1, (2,), last)
    oo_got.append(send(b_cut, to_outer))
    kept_b, sent_b = products([[left_b]], rights, last)
    last = update(
        kept_oi, sent_oi, (oi_rows, 0), (oi_rows, near), (oi_got, 0), (oi_got, near), kept_b
    )
    for k, (kept, sent) in enumerate(((kept_a, sent_a), (kept_b, sent_b))):
        low, low_got = oo_halves[k], oo_got[k]
        last = update(kept, sent, (low, 0), (low, far), (low_got, 0), (low_got, far), last)

    groups, sizes = [], []
    for members in (biases[:4], biases[4:]):
        joined = jnp.concatenate(members, axis=1)
        others = [send(joined, [(i, (i + d) % 4) for i in range(4)]) for d in range(1, 4)]
        groups.append([joined] + others)
        sizes.append([2 * v.shape[1] for v in members])
    table = bias_table(groups, sizes, scalars, heads, count)

    att_w = jnp.swapaxes(att_in, 1, 2).astype(F32) * jnp.array([1, 1, 1, 0.5], F32).reshape(4, 1, 1)
    att_w = att_w.astype(BF16).reshape(4 * chan, chan)
    output = None
    for index in range(own // BLOCK):
        got = list(attention(index, scalars, table, column(gain_att), att_w, att_out.T, pieces))
        for d in range(1, 4):
            got[d] = send(got[d], [(i, (i + d) % 4) for i in range(4)])
        output = place(got, output, index, scalars)
    return output[None]


def solution(mesh):
    in_specs = (
        P(("groups", "dp"), "wide", None, None),
        P(("groups", "dp")),
        P(),
        P(),
        P(),
        P(),
        P(),
        P(),
        P(),
        P(),
        P(),
    )
    out_specs = P(("groups", "dp"), "wide", None, None)
    body = line_body if mesh.shape["wide"] == 4 else general_body
    return jax.shard_map(body, mesh=mesh, in_specs=in_specs, out_specs=out_specs, check_vma=False)
```

profile of v0, /device:TPU:0, one launch (start us, length us, event | category | flops | bytes accessed | tf_op | source)
XLA Modules:
  0.0 397.6 jit_solution(1992078405881394426)
XLA Ops:
  0.0 2.8 collective-permute-start.4
  2.8 4.7 %slice_bitcast_fusion = (bf16[32,256,128]{2,1,0:T(8,128)(2,1)}, bf16[32,256,128]{2,1,0:T(8,128)(2,1)}) fusion(bf16[1,64,256,128]{3,2,1,0:T(8,128)(2,1)} %param.14), kind=kLoop, calls=%fused_computation | loop fusion | bytes 8388608 | tf_op jit(solution)/shard_map/slice | solution.py:595
  7.5 7.1 %collective-permute-start = (bf16[32,256,128]{2,1,0:T(8,128)(2,1)}, bf16[32,256,128]{2,1,0:T(8,128)(2,1)}, u32[]{:S(2)}, u32[]{:S(2)}) collective-permute-start(bf16[32,256,128]{2,1,0:T(8,128)(2,1)} %get-tuple-element.138), channel_id=1, source_target_pairs={{0,4},{12,8},{1,5},{13,9},{2,6},{14,10},{3,7},{15,11},{16,20},{28,... | collective-permute-start | bytes 6291464 | tf_op jit(solution)/shard_map/ppermute | solution.py:586
  21.2 3.2 concatenate.9.refs_0_.refs_4_.refs_6_.refs_5_.scalars
  24.4 16.3 %shard_map.118 = (bf16[128,64,256]{2,1,0:T(8,128)(2,1)}, bf16[128,64,256]{2,1,0:T(8,128)(2,1)}, bf16[64,64,128]{2,1,0:T(8,128)(2,1)}, bf16[64,64,128]{2,1,0:T(8,128)(2,1)}) custom-call(s32[29]{0:T(128)} %concatenate.9.refs_0_.refs_4_.refs_6_.refs_5_.scalars, bf16[64,256,128]{2,1,0:T(8,128)(2,1)} %bitcast.33, f32[128,1]{1,0:T(8,128)} %copy.19.refs_2_.refs_7_, ...), custom_call_target="tpu_custom_call" | custom-call | flops 1024 | bytes 1024 | tf_op jit(solution)/shard_map/pallas_call | solution.py:199
  40.7 18.9 %collective-permute-done.refs_0_ = bf16[32,256,128]{2,1,0:T(8,128)(2,1)} collective-permute-done((bf16[32,256,128]{2,1,0:T(8,128)(2,1)}, bf16[32,256,128]{2,1,0:T(8,128)(2,1)}, u32[]{:S(2)}, u32[]{:S(2)}) %collective-permute-start) | collective-permute-done | bytes 2097184 | tf_op jit(solution)/shard_map/ppermute | solution.py:586
  59.6 2.0 collective-permute-start.5
  61.6 9.7 %shard_map.120 = (bf16[128,32,256]{2,1,0:T(8,128)(2,1)}, bf16[128,32,256]{2,1,0:T(8,128)(2,1)}) custom-call(s32[29]{0:T(128)} %concatenate.9.refs_0_.refs_4_.refs_6_.refs_5_.scalars, bf16[32,256,128]{2,1,0:T(8,128)(2,1)} %shard_map.119.refs_1_.refs_3_, f32[128,1]{1,0:T(8,128)} %copy.19.refs_2_.refs_7_, bf16[512,128]{1,0:T(8,128)(2,1)} %bitcast.41, ...), custom_call_target="tpu_custom_call" | custom-call | flops 1024 | bytes 1024 | tf_op jit(solution)/shard_map/pallas_call | solution.py:199
  71.2 31.8 %collective-permute-done.1.refs_0_ = bf16[32,256,128]{2,1,0:T(8,128)(2,1)S(1)} collective-permute-done((bf16[32,256,128]{2,1,0:T(8,128)(2,1)}, bf16[32,256,128]{2,1,0:T(8,128)(2,1)S(1)}, u32[]{:S(2)}, u32[]{:S(2)}) %collective-permute-start.1) | collective-permute-done | bytes 2097184 | tf_op jit(solution)/shard_map/ppermute | solution.py:586
  106.5 9.7 %shard_map.122 = (bf16[128,32,256]{2,1,0:T(8,128)(2,1)}, bf16[128,32,256]{2,1,0:T(8,128)(2,1)}) custom-call(s32[29]{0:T(128)} %concatenate.9.refs_0_.refs_4_.refs_6_.refs_5_.scalars, bf16[32,256,128]{2,1,0:T(8,128)(2,1)} %shard_map.121.refs_1_.refs_4_, f32[128,1]{1,0:T(8,128)} %copy.19.refs_2_.refs_7_, bf16[512,128]{1,0:T(8,128)(2,1)} %bitcast.42, ...), custom_call_target="tpu_custom_call" | custom-call | flops 1024 | bytes 1024 | tf_op jit(solution)/shard_map/pallas_call | solution.py:199
  116.2 10.7 %shard_map.123 = (bf16[128,32,128]{2,1,0:T(8,128)(2,1)}, bf16[128,32,128]{2,1,0:T(8,128)(2,1)}, bf16[128,32,128]{2,1,0:T(8,128)(2,1)}, bf16[128,32,128]{2,1,0:T(8,128)(2,1)}) custom-call(bf16[128,64,256]{2,1,0:T(8,128)(2,1)} %get-tuple-element.80.refs_1_.refs_0_, bf16[128,32,256]{2,1,0:T(8,128)(2,1)} %get-tuple-element.81.refs_1_.refs_4_, ...), custom_call_target="tpu_custom_call" | custom-call | flops 1024 | bytes 1024 | tf_op jit(solution)/shard_map/pallas_call | solution.py:247
  130.3 11.4 %shard_map.124 = (bf16[128,64,256]{2,1,0:T(8,128)(2,1)}, bf16[64,64,128]{2,1,0:T(8,128)(2,1)}) custom-call(s32[29]{0:T(128)} %concatenate.9.refs_0_.refs_4_.refs_6_.refs_5_.scalars, bf16[64,256,128]{2,1,0:T(8,128)(2,1)} %collective-permute-done.4.refs_1_.refs_3_.refs_4_, f32[128,1]{1,0:T(8,128)} %copy.19.refs_2_.refs_7_, bf16[256,128]{1,0:T(8,128)(2,1)} %bitcast.43, ...), custom_call_target="tpu_custom_call" | custom-call | flops 1024 | bytes 1024 | tf_op jit(solution)/shard_map/pallas_call | solution.py:199
  141.6 7.3 %shard_map.125 = (bf16[128,32,256]{2,1,0:T(8,128)(2,1)}, bf16[32,64,128]{2,1,0:T(8,128)(2,1)}) custom-call(s32[29]{0:T(128)} %concatenate.9.refs_0_.refs_4_.refs_6_.refs_5_.scalars, bf16[32,256,128]{2,1,0:T(8,128)(2,1)} %collective-permute-done.5.refs_1_.refs_3_.refs_4_, f32[128,1]{1,0:T(8,128)} %copy.19.refs_2_.refs_7_, bf16[256,128]{1,0:T(8,128)(2,1)} %bitcast.44, ...), custom_call_target="tpu_custom_call" | custom-call | flops 1024 | bytes 1024 | tf_op jit(solution)/shard_map/pallas_call | solution.py:199
  148.9 10.2 %shard_map.126 = (bf16[128,32,128]{2,1,0:T(8,128)(2,1)}, bf16[128,32,128]{2,1,0:T(8,128)(2,1)}, bf16[128,16,128]{2,1,0:T(8,128)(2,1)}, bf16[128,16,128]{2,1,0:T(8,128)(2,1)}) custom-call(bf16[128,64,256]{2,1,0:T(8,128)(2,1)} %get-tuple-element.90.refs_4_.refs_0_, bf16[128,32,256]{2,1,0:T(8,128)(2,1)} %get-tuple-element.91.refs_1_, ...), custom_call_target="tpu_custom_call" | custom-call | flops 1024 | bytes 1024 | tf_op jit(solution)/shard_map/pallas_call | solution.py:247
  166.9 8.5 %shard_map.127 = (bf16[32,64,128]{2,1,0:T(8,128)(2,1)}, bf16[32,64,128]{2,1,0:T(8,128)(2,1)}, bf16[4,32,128]{2,1,0:T(8,128)(2,1)}) custom-call(s32[29]{0:T(128)} %concatenate.9.refs_0_.refs_4_.refs_6_.refs_5_.scalars, bf16[128,32,128]{2,1,0:T(8,128)(2,1)} %get-tuple-element.86.refs_1_, bf16[128,32,128]{2,1,0:T(8,128)(2,1)} %collective-permute-done.2.refs_2_, ...), custom_call_target="tpu_custom_call" | custom-call | flops 1024 | bytes 1024 | tf_op jit(solution)/shard_map/pallas_call | solution.py:342
  175.4 3.6 collective-permute-done.6.refs_2_
  180.5 8.5 %shard_map.128 = (bf16[32,64,128]{2,1,0:T(8,128)(2,1)}, bf16[32,64,128]{2,1,0:T(8,128)(2,1)}, bf16[4,32,128]{2,1,0:T(8,128)(2,1)}) custom-call(s32[29]{0:T(128)} %concatenate.9.refs_0_.refs_4_.refs_6_.refs_5_.scalars, bf16[128,32,128]{2,1,0:T(8,128)(2,1)} %get-tuple-element.89.refs_4_.refs_1_, bf16[128,32,128]{2,1,0:T(8,128)(2,1)} %collective-permute-done.6.refs_2_, ...), custom_call_target="tpu_custom_call" | custom-call | flops 1024 | bytes 1024 | tf_op jit(solution)/shard_map/pallas_call | solution.py:342
  190.4 7.2 %shard_map.129 = (bf16[128,32,256]{2,1,0:T(8,128)(2,1)}, bf16[32,64,128]{2,1,0:T(8,128)(2,1)}) custom-call(s32[29]{0:T(128)} %concatenate.9.refs_0_.refs_4_.refs_6_.refs_5_.scalars, bf16[32,256,128]{2,1,0:T(8,128)(2,1)} %copy-done.1, f32[128,1]{1,0:T(8,128)} %copy.19.refs_2_.refs_7_, bf16[256,128]{1,0:T(8,128)(2,1)} %bitcast.45, ...), custom_call_target="tpu_custom_call" | custom-call | flops 1024 | bytes 1024 | tf_op jit(solution)/shard_map/pallas_call | solution.py:199
  197.6 9.0 %shard_map.130 = (bf16[128,16,128]{2,1,0:T(8,128)(2,1)}, bf16[128,16,128]{2,1,0:T(8,128)(2,1)}) custom-call(bf16[128,32,256]{2,1,0:T(8,128)(2,1)} %get-tuple-element.99.refs_0_, bf16[128,64,256]{2,1,0:T(8,128)(2,1)} %get-tuple-element.83.refs_3_.refs_2_.refs_1_, bf16[128,32,256]{2,1,0:T(8,128)(2,1)} %get-tuple-element.84.refs_4_.refs_3_.refs_2_, ...), custom_call_target="tpu_custom_call" | custom-call | flops 1024 | bytes 1024 | tf_op jit(solution)/shard_map/pallas_call | solution.py:247
  209.2 14.7 %collective-permute-done.8.refs_5_.refs_6_ = bf16[64,64,128]{2,1,0:T(8,128)(2,1)S(1)} collective-permute-done((bf16[64,64,128]{2,1,0:T(8,128)(2,1)}, bf16[64,64,128]{2,1,0:T(8,128)(2,1)S(1)}, u32[]{:S(2)}, u32[]{:S(2)}) %collective-permute-start.8) | collective-permute-done | bytes 1048608 | tf_op jit(solution)/shard_map/ppermute | solution.py:586
  224.9 8.5 %shard_map.131 = (bf16[32,64,128]{2,1,0:T(8,128)(2,1)}, bf16[32,64,128]{2,1,0:T(8,128)(2,1)}, bf16[4,32,128]{2,1,0:T(8,128)(2,1)}) custom-call(s32[29]{0:T(128)} %concatenate.9.refs_0_.refs_4_.refs_6_.refs_5_.scalars, bf16[128,32,128]{2,1,0:T(8,128)(2,1)} %get-tuple-element.92.refs_13_.refs_1_, bf16[128,32,128]{2,1,0:T(8,128)(2,1)} %collective-permute-done.7.refs_2_, ...), custom_call_target="tpu_custom_call" | custom-call | flops 1024 | bytes 1024 | tf_op jit(solution)/shard_map/pallas_call | solution.py:342
  233.3 1.9 collective-permute-done.10.refs_2_
  235.2 11.1 %collective-permute-done.11.refs_5_.refs_6_ = bf16[32,64,128]{2,1,0:T(8,128)(2,1)S(1)} collective-permute-done((bf16[32,64,128]{2,1,0:T(8,128)(2,1)}, bf16[32,64,128]{2,1,0:T(8,128)(2,1)S(1)}, u32[]{:S(2)}, u32[]{:S(2)}) %collective-permute-start.11) | collective-permute-done | bytes 524320 | tf_op jit(solution)/shard_map/ppermute | solution.py:586
  247.2 5.6 %shard_map.132 = (bf16[16,64,128]{2,1,0:T(8,128)(2,1)}, bf16[16,64,128]{2,1,0:T(8,128)(2,1)}, bf16[4,16,128]{2,1,0:T(8,128)(2,1)}) custom-call(s32[29]{0:T(128)} %concatenate.9.refs_0_.refs_4_.refs_6_.refs_5_.scalars, bf16[128,16,128]{2,1,0:T(8,128)(2,1)} %get-tuple-element.102.refs_1_, bf16[128,16,128]{2,1,0:T(8,128)(2,1)} %collective-permute-done.10.refs_2_, ...), custom_call_target="tpu_custom_call" | custom-call | flops 1024 | bytes 1024 | tf_op jit(solution)/shard_map/pallas_call | solution.py:342
  252.7 4.8 %collective-permute-done.15.refs_2_ = bf16[128,16,128]{2,1,0:T(8,128)(2,1)S(1)} collective-permute-done((bf16[128,16,128]{2,1,0:T(8,128)(2,1)}, bf16[128,16,128]{2,1,0:T(8,128)(2,1)S(1)}, u32[]{:S(2)}, u32[]{:S(2)}) %collective-permute-start.15) | collective-permute-done | bytes 524320 | tf_op jit(solution)/shard_map/ppermute | solution.py:586
  257.6 9.7 %collective-permute-done.16.refs_5_.refs_6_ = bf16[32,64,128]{2,1,0:T(8,128)(2,1)S(1)} collective-permute-done((bf16[32,64,128]{2,1,0:T(8,128)(2,1)S(1)}, bf16[32,64,128]{2,1,0:T(8,128)(2,1)S(1)}, u32[]{:S(2)}, u32[]{:S(2)}) %collective-permute-start.16) | collective-permute-done | bytes 524320 | tf_op jit(solution)/shard_map/ppermute | solution.py:586
  268.1 5.7 %shard_map.133 = (bf16[16,64,128]{2,1,0:T(8,128)(2,1)}, bf16[16,64,128]{2,1,0:T(8,128)(2,1)}, bf16[4,16,128]{2,1,0:T(8,128)(2,1)}) custom-call(s32[29]{0:T(128)} %concatenate.9.refs_0_.refs_4_.refs_6_.refs_5_.scalars, bf16[128,16,128]{2,1,0:T(8,128)(2,1)} %get-tuple-element.100.refs_13_.refs_1_, bf16[128,16,128]{2,1,0:T(8,128)(2,1)} %copy-done.6, ...), custom_call_target="tpu_custom_call" | custom-call | flops 1024 | bytes 1024 | tf_op jit(solution)/shard_map/pallas_call | solution.py:342
  273.8 3.0 collective-permute-start.18
  279.8 2.8 collective-permute-start.14
  285.2 3.0 collective-permute-done.13.refs_2_
  289.5 3.2 shard_map.134.table
  292.7 13.6 %shard_map.138 = (bf16[64,16,128]{2,1,0:T(8,128)(2,1)}, bf16[64,16,128]{2,1,0:T(8,128)(2,1)}, bf16[64,16,128]{2,1,0:T(8,128)(2,1)}, bf16[64,16,128]{2,1,0:T(8,128)(2,1)}) custom-call(s32[29]{0:T(128)} %concatenate.9.refs_0_.refs_4_.refs_6_.refs_5_.scalars, f32[4,256,256]{2,1,0:T(8,128)} %shard_map.134.table, f32[128,1]{1,0:T(8,128)} %copy.29.refs_9_.gain_ref, ...), custom_call_target="tpu_custom_call" | custom-call | flops 1024 | bytes 1024 | tf_op jit(solution)/shard_map/pallas_call | solution.py:492
  307.9 2.1 collective-permute-start.30
  310.3 13.6 %shard_map.137 = (bf16[64,16,128]{2,1,0:T(8,128)(2,1)}, bf16[64,16,128]{2,1,0:T(8,128)(2,1)}, bf16[64,16,128]{2,1,0:T(8,128)(2,1)}, bf16[64,16,128]{2,1,0:T(8,128)(2,1)}) custom-call(s32[29]{0:T(128)} %concatenate.9.refs_0_.refs_4_.refs_6_.refs_5_.scalars, f32[4,256,256]{2,1,0:T(8,128)} %shard_map.134.table, f32[128,1]{1,0:T(8,128)} %copy.29.refs_9_.gain_ref, ...), custom_call_target="tpu_custom_call" | custom-call | flops 1024 | bytes 1024 | tf_op jit(solution)/shard_map/pallas_call | solution.py:492
  324.0 1.7 collective-permute-start.26
  326.5 13.6 %shard_map.136 = (bf16[64,16,128]{2,1,0:T(8,128)(2,1)}, bf16[64,16,128]{2,1,0:T(8,128)(2,1)}, bf16[64,16,128]{2,1,0:T(8,128)(2,1)}, bf16[64,16,128]{2,1,0:T(8,128)(2,1)}) custom-call(s32[29]{0:T(128)} %concatenate.9.refs_0_.refs_4_.refs_6_.refs_5_.scalars, f32[4,256,256]{2,1,0:T(8,128)} %shard_map.134.table, f32[128,1]{1,0:T(8,128)} %copy.29.refs_9_.gain_ref, ...), custom_call_target="tpu_custom_call" | custom-call | flops 1024 | bytes 1024 | tf_op jit(solution)/shard_map/pallas_call | solution.py:492
  340.1 2.3 collective-permute-start.28
  342.5 13.8 %shard_map.135 = (bf16[64,16,128]{2,1,0:T(8,128)(2,1)}, bf16[64,16,128]{2,1,0:T(8,128)(2,1)}, bf16[64,16,128]{2,1,0:T(8,128)(2,1)}, bf16[64,16,128]{2,1,0:T(8,128)(2,1)}) custom-call(s32[29]{0:T(128)} %concatenate.9.refs_0_.refs_4_.refs_6_.refs_5_.scalars, f32[4,256,256]{2,1,0:T(8,128)} %shard_map.134.table, f32[128,1]{1,0:T(8,128)} %copy.29.refs_9_.gain_ref, ...), custom_call_target="tpu_custom_call" | custom-call | flops 1024 | bytes 1024 | tf_op jit(solution)/shard_map/pallas_call | solution.py:492
  356.3 1.8 collective-permute-start.24
  358.1 2.1 collective-permute-start.25
  360.8 2.4 collective-permute-start.21
  363.1 3.7 collective-permute-start.22
  366.9 2.8 shard_map.139.refs_4_
  369.8 2.8 shard_map.140.refs_4_
  372.6 8.1 %collective-permute-done.24.refs_2_ = bf16[64,16,128]{2,1,0:T(8,128)(2,1)S(1)} collective-permute-done((bf16[64,16,128]{2,1,0:T(8,128)(2,1)S(1)}, bf16[64,16,128]{2,1,0:T(8,128)(2,1)S(1)}, u32[]{:S(2)}, u32[]{:S(2)}) %collective-permute-start.24) | collective-permute-done | bytes 262176 | tf_op jit(solution)/shard_map/ppermute | solution.py:586
  381.5 2.8 shard_map.141.refs_4_
  384.4 9.4 %collective-permute-done.21.refs_2_ = bf16[64,16,128]{2,1,0:T(8,128)(2,1)S(1)} collective-permute-done((bf16[64,16,128]{2,1,0:T(8,128)(2,1)}, bf16[64,16,128]{2,1,0:T(8,128)(2,1)S(1)}, u32[]{:S(2)}, u32[]{:S(2)}) %collective-permute-start.21) | collective-permute-done | bytes 262176 | tf_op jit(solution)/shard_map/ppermute | solution.py:586
  394.6 2.8 shard_map.142
  (156 shorter events, 40.0 us)
Async XLA Ops:
  0.0 16.1 %copy-start.23 = (bf16[4,128,128]{2,1,0:T(8,128)(2,1)S(1)}, bf16[4,128,128]{2,1,0:T(8,128)(2,1)}, u32[]{:S(2)}) copy-start(bf16[4,128,128]{2,1,0:T(8,128)(2,1)} %param.17) | copy-start | bytes 393220
  0.0 16.8 %copy-start.36 = (f32[128]{0:T(128)S(1)}, f32[128]{0:T(128)}, u32[]{:S(2)}) copy-start(f32[128]{0:T(128)} %param.16) | copy-start | bytes 1540
  0.0 128.2 %collective-permute-start.4 = (bf16[64,256,128]{2,1,0:T(8,128)(2,1)}, bf16[64,256,128]{2,1,0:T(8,128)(2,1)}, u32[]{:S(2)}, u32[]{:S(2)}) collective-permute-start(bf16[64,256,128]{2,1,0:T(8,128)(2,1)} %bitcast.32), channel_id=1, source_target_pairs={{4,8},{8,4},{5,9},{9,5},{6,10},{10,6},{7,11},{11,7},{20,24},{24,20... | collective-permute-start | bytes 12582920 | tf_op jit(solution)/shard_map/ppermute | solution.py:586
  7.5 52.1 %collective-permute-start = (bf16[32,256,128]{2,1,0:T(8,128)(2,1)}, bf16[32,256,128]{2,1,0:T(8,128)(2,1)}, u32[]{:S(2)}, u32[]{:S(2)}) collective-permute-start(bf16[32,256,128]{2,1,0:T(8,128)(2,1)} %get-tuple-element.138), channel_id=1, source_target_pairs={{0,4},{12,8},{1,5},{13,9},{2,6},{14,10},{3,7},{15,11},{16,20},{28,... | collective-permute-start | bytes 6291464 | tf_op jit(solution)/shard_map/ppermute | solution.py:586
  14.5 88.5 %collective-permute-start.1 = (bf16[32,256,128]{2,1,0:T(8,128)(2,1)}, bf16[32,256,128]{2,1,0:T(8,128)(2,1)S(1)}, u32[]{:S(2)}, u32[]{:S(2)}) collective-permute-start(bf16[32,256,128]{2,1,0:T(8,128)(2,1)} %get-tuple-element.137), channel_id=1, source_target_pairs={{0,4},{12,8},{1,5},{13,9},{2,6},{14,10},{3,7},{15,11},{16,20},{28,... | collective-permute-start | bytes 6291464 | tf_op jit(solution)/shard_map/ppermute | solution.py:586
  59.6 82.1 %collective-permute-start.5 = (bf16[32,256,128]{2,1,0:T(8,128)(2,1)}, bf16[32,256,128]{2,1,0:T(8,128)(2,1)}, u32[]{:S(2)}, u32[]{:S(2)}) collective-permute-start(bf16[32,256,128]{2,1,0:T(8,128)(2,1)} %shard_map.119.refs_1_.refs_3_), channel_id=1, source_target_pairs={{4,8},{8,4},{5,9},{9,5},{6,10},{10,6},{7,11},{11,7},{20,24},{24,20... | collective-permute-start | bytes 6291464 | tf_op jit(solution)/shard_map/ppermute | solution.py:586
  104.4 84.6 %collective-permute-start.9 = (bf16[32,256,128]{2,1,0:T(8,128)(2,1)}, bf16[32,256,128]{2,1,0:T(8,128)(2,1)S(1)}, u32[]{:S(2)}, u32[]{:S(2)}) collective-permute-start(bf16[32,256,128]{2,1,0:T(8,128)(2,1)} %shard_map.121.refs_1_.refs_4_), channel_id=1, source_target_pairs={{4,8},{8,4},{5,9},{9,5},{6,10},{10,6},{7,11},{11,7},{20,24},{24,20... | collective-permute-start | bytes 6291464 | tf_op jit(solution)/shard_map/ppermute | solution.py:586
  105.2 55.2 %collective-permute-start.3 = (bf16[64,64,128]{2,1,0:T(8,128)(2,1)}, bf16[64,64,128]{2,1,0:T(8,128)(2,1)S(1)}, u32[]{:S(2)}, u32[]{:S(2)}) collective-permute-start(bf16[64,64,128]{2,1,0:T(8,128)(2,1)} %get-tuple-element.88), channel_id=1, source_target_pairs={{4,0},{8,12},{5,1},{9,13},{6,2},{10,14},{7,3},{11,15},{20,16},{24,... | collective-permute-start | bytes 3145736 | tf_op jit(solution)/shard_map/ppermute | solution.py:586
  126.9 38.7 %collective-permute-start.2 = (bf16[128,32,128]{2,1,0:T(8,128)(2,1)}, bf16[128,32,128]{2,1,0:T(8,128)(2,1)}, u32[]{:S(2)}, u32[]{:S(2)}) collective-permute-start(bf16[128,32,128]{2,1,0:T(8,128)(2,1)} %get-tuple-element.87), channel_id=1, source_target_pairs={{4,0},{8,12},{5,1},{9,13},{6,2},{10,14},{7,3},{11,15},{20,16},{24,... | collective-permute-start | bytes 3145736 | tf_op jit(solution)/shard_map/ppermute | solution.py:586
  128.2 50.8 %collective-permute-start.6 = (bf16[128,32,128]{2,1,0:T(8,128)(2,1)}, bf16[128,32,128]{2,1,0:T(8,128)(2,1)}, u32[]{:S(2)}, u32[]{:S(2)}) collective-permute-start(bf16[128,32,128]{2,1,0:T(8,128)(2,1)} %get-tuple-element.94), channel_id=1, source_target_pairs={{4,0},{8,12},{5,1},{9,13},{6,2},{10,14},{7,3},{11,15},{20,16},{24,... | collective-permute-start | bytes 3145736 | tf_op jit(solution)/shard_map/ppermute | solution.py:586
  148.9 13.8 %copy-start.37 = (f32[128]{0:T(128)S(1)}, f32[128]{0:T(128)}, u32[]{:S(2)}) copy-start(f32[128]{0:T(128)} %param.21) | copy-start | bytes 1540
  148.9 14.5 %copy-start.29 = (bf16[128,128]{1,0:T(8,128)(2,1)S(1)}, bf16[128,128]{1,0:T(8,128)(2,1)}, u32[]{:S(2)}) copy-start(bf16[128,128]{1,0:T(8,128)(2,1)} %param.20) | copy-start | bytes 98308
  148.9 14.6 %copy-start.30 = (bf16[128,128]{1,0:T(8,128)(2,1)S(1)}, bf16[128,128]{1,0:T(8,128)(2,1)}, u32[]{:S(2)}) copy-start(bf16[128,128]{1,0:T(8,128)(2,1)} %param.18) | copy-start | bytes 98308
  148.9 14.8 %copy-start.38 = (f32[128]{0:T(128)S(1)}, f32[128]{0:T(128)}, u32[]{:S(2)}) copy-start(f32[128]{0:T(128)} %param.19) | copy-start | bytes 1540
  148.9 15.5 %copy-start.35 = (bf16[128,4]{0,1:T(4,128)(2,1)S(1)}, bf16[128,4]{0,1:T(4,128)(2,1)}, u32[]{:S(2)}) copy-start(bf16[128,4]{0,1:T(4,128)(2,1)} %param.23) | copy-start | bytes 3076
  159.1 48.7 %collective-permute-start.7 = (bf16[128,32,128]{2,1,0:T(8,128)(2,1)}, bf16[128,32,128]{2,1,0:T(8,128)(2,1)}, u32[]{:S(2)}, u32[]{:S(2)}) collective-permute-start(bf16[128,32,128]{2,1,0:T(8,128)(2,1)} %get-tuple-element.97), channel_id=1, source_target_pairs={{4,0},{8,12},{5,1},{9,13},{6,2},{10,14},{7,3},{11,15},{20,16},{24,... | collective-permute-start | bytes 3145736 | tf_op jit(solution)/shard_map/ppermute | solution.py:586
  161.4 62.5 %collective-permute-start.8 = (bf16[64,64,128]{2,1,0:T(8,128)(2,1)}, bf16[64,64,128]{2,1,0:T(8,128)(2,1)S(1)}, u32[]{:S(2)}, u32[]{:S(2)}) collective-permute-start(bf16[64,64,128]{2,1,0:T(8,128)(2,1)} %get-tuple-element.98), channel_id=1, source_target_pairs={{4,0},{8,12},{5,1},{9,13},{6,2},{10,14},{7,3},{11,15},{20,16},{24,... | collective-permute-start | bytes 3145736 | tf_op jit(solution)/shard_map/ppermute | solution.py:586
  165.7 69.6 %collective-permute-start.10 = (bf16[128,16,128]{2,1,0:T(8,128)(2,1)}, bf16[128,16,128]{2,1,0:T(8,128)(2,1)}, u32[]{:S(2)}, u32[]{:S(2)}) collective-permute-start(bf16[128,16,128]{2,1,0:T(8,128)(2,1)} %get-tuple-element.103), channel_id=1, source_target_pairs={{4,0},{8,12},{5,1},{9,13},{6,2},{10,14},{7,3},{11,15},{20,16},{24,... | collective-permute-start | bytes 1572872 | tf_op jit(solution)/shard_map/ppermute | solution.py:586
  179.1 67.3 %collective-permute-start.11 = (bf16[32,64,128]{2,1,0:T(8,128)(2,1)}, bf16[32,64,128]{2,1,0:T(8,128)(2,1)S(1)}, u32[]{:S(2)}, u32[]{:S(2)}) collective-permute-start(bf16[32,64,128]{2,1,0:T(8,128)(2,1)} %get-tuple-element.104), channel_id=1, source_target_pairs={{4,0},{8,12},{5,1},{9,13},{6,2},{10,14},{7,3},{11,15},{20,16},{24,... | collective-permute-start | bytes 1572872 | tf_op jit(solution)/shard_map/ppermute | solution.py:586
  197.5 11.6 %copy-start.7 = (bf16[4,32,128]{2,1,0:T(8,128)(2,1)S(1)}, bf16[4,32,128]{2,1,0:T(8,128)(2,1)}, u32[]{:S(2)}) copy-start(bf16[4,32,128]{2,1,0:T(8,128)(2,1)} %get-tuple-element.96.refs_4_) | copy-start | bytes 98308
  206.5 51.0 %collective-permute-start.15 = (bf16[128,16,128]{2,1,0:T(8,128)(2,1)}, bf16[128,16,128]{2,1,0:T(8,128)(2,1)S(1)}, u32[]{:S(2)}, u32[]{:S(2)}) collective-permute-start(bf16[128,16,128]{2,1,0:T(8,128)(2,1)} %get-tuple-element.106), channel_id=1, source_target_pairs={{4,0},{8,12},{5,1},{9,13},{6,2},{10,14},{7,3},{11,15},{20,16},{24,... | collective-permute-start | bytes 1572872 | tf_op jit(solution)/shard_map/ppermute | solution.py:586
  207.9 59.4 %collective-permute-start.16 = (bf16[32,64,128]{2,1,0:T(8,128)(2,1)S(1)}, bf16[32,64,128]{2,1,0:T(8,128)(2,1)S(1)}, u32[]{:S(2)}, u32[]{:S(2)}) collective-permute-start(bf16[32,64,128]{2,1,0:T(8,128)(2,1)S(1)} %copy-done.40), channel_id=1, source_target_pairs={{4,0},{8,12},{5,1},{9,13},{6,2},{10,14},{7,3},{11,15},{20,16},{24,... | collective-permute-start | bytes 1572872 | tf_op jit(solution)/shard_map/ppermute | solution.py:586
  268.1 14.6 %copy-start.24 = (bf16[4,128,128]{2,1,0:T(8,128)(2,1)S(1)}, bf16[4,128,128]{2,1,0:T(8,128)(2,1)}, u32[]{:S(2)}) copy-start(bf16[4,128,128]{2,1,0:T(8,128)(2,1)} %param.22) | copy-start | bytes 393220
  268.1 14.6 %copy-start.39 = (f32[4]{0:T(128)S(1)}, f32[4]{0:T(128)}, u32[]{:S(2)}) copy-start(f32[4]{0:T(128)} %constant.97.clone) | copy-start | bytes 52
  268.1 15.4 %copy-start.31 = (bf16[128,128]{1,0:T(8,128)(2,1)S(1)}, bf16[128,128]{1,0:T(8,128)(2,1)}, u32[]{:S(2)}) copy-start(bf16[128,128]{1,0:T(8,128)(2,1)} %param.24) | copy-start | bytes 98308
  273.8 6.0 %collective-permute-start.17 = (bf16[4,16,128]{2,1,0:T(8,128)(2,1)}, bf16[4,16,128]{2,1,0:T(8,128)(2,1)S(1)}, u32[]{:S(2)}, u32[]{:S(2)}) collective-permute-start(bf16[4,16,128]{2,1,0:T(8,128)(2,1)} %get-tuple-element.108.refs_4_), channel_id=1, source_target_pairs={{0,4},{4,8},{8,12},{12,0},{1,5},{5,9},{9,13},{13,1},{2,6},{6,10},{... | collective-permute-start | bytes 49160 | tf_op jit(solution)/shard_map/ppermute | solution.py:586
  273.8 10.5 %collective-permute-start.18 = (bf16[4,16,128]{2,1,0:T(8,128)(2,1)}, bf16[4,16,128]{2,1,0:T(8,128)(2,1)S(1)}, u32[]{:S(2)}, u32[]{:S(2)}) collective-permute-start(bf16[4,16,128]{2,1,0:T(8,128)(2,1)} %get-tuple-element.108.refs_4_), channel_id=1, source_target_pairs={{0,8},{4,12},{8,0},{12,4},{1,9},{5,13},{9,1},{13,5},{2,10},{6,14},... | collective-permute-start | bytes 49160 | tf_op jit(solution)/shard_map/ppermute | solution.py:586
  276.8 7.4 %collective-permute-start.19 = (bf16[4,16,128]{2,1,0:T(8,128)(2,1)}, bf16[4,16,128]{2,1,0:T(8,128)(2,1)S(1)}, u32[]{:S(2)}, u32[]{:S(2)}) collective-permute-start(bf16[4,16,128]{2,1,0:T(8,128)(2,1)} %get-tuple-element.108.refs_4_), channel_id=1, source_target_pairs={{0,12},{4,0},{8,4},{12,8},{1,13},{5,1},{9,5},{13,9},{2,14},{6,2},{... | collective-permute-start | bytes 49160 | tf_op jit(solution)/shard_map/ppermute | solution.py:586
  277.6 7.6 %collective-permute-start.12 = (bf16[4,112,128]{2,1,0:T(8,128)(2,1)S(1)}, bf16[4,112,128]{2,1,0:T(8,128)(2,1)S(1)}, u32[]{:S(2)}, u32[]{:S(2)}) collective-permute-start(bf16[4,112,128]{2,1,0:T(8,128)(2,1)S(1)} %constant_dynamic-update-slice_fusion.refs_0_), channel_id=1, source_target_pairs={{0,4},{4,8},{8,12},{12,0},{1,5},{5,9},{9,13},{13,1},{2,6},{6,10},{... | collective-permute-start | bytes 344072 | tf_op jit(solution)/shard_map/ppermute | solution.py:586
  278.9 9.3 %collective-permute-start.13 = (bf16[4,112,128]{2,1,0:T(8,128)(2,1)S(1)}, bf16[4,112,128]{2,1,0:T(8,128)(2,1)S(1)}, u32[]{:S(2)}, u32[]{:S(2)}) collective-permute-start(bf16[4,112,128]{2,1,0:T(8,128)(2,1)S(1)} %constant_dynamic-update-slice_fusion.refs_0_), channel_id=1, source_target_pairs={{0,8},{4,12},{8,0},{12,4},{1,9},{5,13},{9,1},{13,5},{2,10},{6,14},... | collective-permute-start | bytes 344072 | tf_op jit(solution)/shard_map/ppermute | solution.py:586
  279.8 8.4 %collective-permute-start.14 = (bf16[4,112,128]{2,1,0:T(8,128)(2,1)S(1)}, bf16[4,112,128]{2,1,0:T(8,128)(2,1)S(1)}, u32[]{:S(2)}, u32[]{:S(2)}) collective-permute-start(bf16[4,112,128]{2,1,0:T(8,128)(2,1)S(1)} %constant_dynamic-update-slice_fusion.refs_0_), channel_id=1, source_target_pairs={{0,12},{4,0},{8,4},{12,8},{1,13},{5,1},{9,5},{13,9},{2,14},{6,2},{... | collective-permute-start | bytes 344072 | tf_op jit(solution)/shard_map/ppermute | solution.py:586
  306.3 33.8 %collective-permute-start.29 = (bf16[64,16,128]{2,1,0:T(8,128)(2,1)}, bf16[64,16,128]{2,1,0:T(8,128)(2,1)S(1)}, u32[]{:S(2)}, u32[]{:S(2)}) collective-permute-start(bf16[64,16,128]{2,1,0:T(8,128)(2,1)} %get-tuple-element.132), channel_id=1, source_target_pairs={{0,4},{4,8},{8,12},{12,0},{1,5},{5,9},{9,13},{13,1},{2,6},{6,10},{... | collective-permute-start | bytes 786440 | tf_op jit(solution)/shard_map/ppermute | solution.py:586
  307.9 34.5 %collective-permute-start.30 = (bf16[64,16,128]{2,1,0:T(8,128)(2,1)}, bf16[64,16,128]{2,1,0:T(8,128)(2,1)S(1)}, u32[]{:S(2)}, u32[]{:S(2)}) collective-permute-start(bf16[64,16,128]{2,1,0:T(8,128)(2,1)} %get-tuple-element.133), channel_id=1, source_target_pairs={{0,8},{4,12},{8,0},{12,4},{1,9},{5,13},{9,1},{13,5},{2,10},{6,14},... | collective-permute-start | bytes 786440 | tf_op jit(solution)/shard_map/ppermute | solution.py:586
  310.0 46.3 %collective-permute-start.31 = (bf16[64,16,128]{2,1,0:T(8,128)(2,1)}, bf16[64,16,128]{2,1,0:T(8,128)(2,1)S(1)}, u32[]{:S(2)}, u32[]{:S(2)}) collective-permute-start(bf16[64,16,128]{2,1,0:T(8,128)(2,1)} %get-tuple-element.134), channel_id=1, source_target_pairs={{0,12},{4,0},{8,4},{12,8},{1,13},{5,1},{9,5},{13,9},{2,14},{6,2},{... | collective-permute-start | bytes 786440 | tf_op jit(solution)/shard_map/ppermute | solution.py:586
  324.0 34.2 %collective-permute-start.26 = (bf16[64,16,128]{2,1,0:T(8,128)(2,1)}, bf16[64,16,128]{2,1,0:T(8,128)(2,1)S(1)}, u32[]{:S(2)}, u32[]{:S(2)}) collective-permute-start(bf16[64,16,128]{2,1,0:T(8,128)(2,1)} %get-tuple-element.128), channel_id=1, source_target_pairs={{0,4},{4,8},{8,12},{12,0},{1,5},{5,9},{9,13},{13,1},{2,6},{6,10},{... | collective-permute-start | bytes 786440 | tf_op jit(solution)/shard_map/ppermute | solution.py:586
  325.7 14.4 %copy-start.43 = (bf16[64,16,128]{2,1,0:T(8,128)(2,1)S(1)}, bf16[64,16,128]{2,1,0:T(8,128)(2,1)}, u32[]{:S(2)}) copy-start(bf16[64,16,128]{2,1,0:T(8,128)(2,1)} %get-tuple-element.130) | copy-start | bytes 786436
  325.7 34.6 %collective-permute-start.27 = (bf16[64,16,128]{2,1,0:T(8,128)(2,1)}, bf16[64,16,128]{2,1,0:T(8,128)(2,1)S(1)}, u32[]{:S(2)}, u32[]{:S(2)}) collective-permute-start(bf16[64,16,128]{2,1,0:T(8,128)(2,1)} %get-tuple-element.129), channel_id=1, source_target_pairs={{0,8},{4,12},{8,0},{12,4},{1,9},{5,13},{9,1},{13,5},{2,10},{6,14},... | collective-permute-start | bytes 786440 | tf_op jit(solution)/shard_map/ppermute | solution.py:586
  340.1 16.2 %copy-start.17 = (bf16[64,16,128]{2,1,0:T(8,128)(2,1)}, bf16[64,16,128]{2,1,0:T(8,128)(2,1)S(1)}, u32[]{:S(2)}) copy-start(bf16[64,16,128]{2,1,0:T(8,128)(2,1)S(1)} %collective-permute-done.29.refs_1_) | copy-start | bytes 786436
  340.1 20.6 %collective-permute-start.28 = (bf16[64,16,128]{2,1,0:T(8,128)(2,1)S(1)}, bf16[64,16,128]{2,1,0:T(8,128)(2,1)S(1)}, u32[]{:S(2)}, u32[]{:S(2)}) collective-permute-start(bf16[64,16,128]{2,1,0:T(8,128)(2,1)S(1)} %copy-done.43), channel_id=1, source_target_pairs={{0,12},{4,0},{8,4},{12,8},{1,13},{5,1},{9,5},{13,9},{2,14},{6,2},{... | collective-permute-start | bytes 786440 | tf_op jit(solution)/shard_map/ppermute | solution.py:586
  342.4 13.8 %copy-start.18 = (bf16[64,16,128]{2,1,0:T(8,128)(2,1)}, bf16[64,16,128]{2,1,0:T(8,128)(2,1)S(1)}, u32[]{:S(2)}) copy-start(bf16[64,16,128]{2,1,0:T(8,128)(2,1)S(1)} %collective-permute-done.30.refs_2_) | copy-start | bytes 786436
  342.4 13.9 %copy-start.42 = (bf16[64,16,128]{2,1,0:T(8,128)(2,1)S(1)}, bf16[64,16,128]{2,1,0:T(8,128)(2,1)}, u32[]{:S(2)}) copy-start(bf16[64,16,128]{2,1,0:T(8,128)(2,1)} %get-tuple-element.125) | copy-start | bytes 786436
  342.4 15.7 %copy-start.41 = (bf16[64,16,128]{2,1,0:T(8,128)(2,1)S(1)}, bf16[64,16,128]{2,1,0:T(8,128)(2,1)}, u32[]{:S(2)}) copy-start(bf16[64,16,128]{2,1,0:T(8,128)(2,1)} %get-tuple-element.126) | copy-start | bytes 786436
  342.4 20.7 %collective-permute-start.23 = (bf16[64,16,128]{2,1,0:T(8,128)(2,1)}, bf16[64,16,128]{2,1,0:T(8,128)(2,1)S(1)}, u32[]{:S(2)}, u32[]{:S(2)}) collective-permute-start(bf16[64,16,128]{2,1,0:T(8,128)(2,1)} %get-tuple-element.124), channel_id=1, source_target_pairs={{0,4},{4,8},{8,12},{12,0},{1,5},{5,9},{9,13},{13,1},{2,6},{6,10},{... | collective-permute-start | bytes 786440 | tf_op jit(solution)/shard_map/ppermute | solution.py:586
  356.3 24.4 %collective-permute-start.24 = (bf16[64,16,128]{2,1,0:T(8,128)(2,1)S(1)}, bf16[64,16,128]{2,1,0:T(8,128)(2,1)S(1)}, u32[]{:S(2)}, u32[]{:S(2)}) collective-permute-start(bf16[64,16,128]{2,1,0:T(8,128)(2,1)S(1)} %copy-done.42), channel_id=1, source_target_pairs={{0,8},{4,12},{8,0},{12,4},{1,9},{5,13},{9,1},{13,5},{2,10},{6,14},... | collective-permute-start | bytes 786440 | tf_op jit(solution)/shard_map/ppermute | solution.py:586
  358.1 22.6 %collective-permute-start.25 = (bf16[64,16,128]{2,1,0:T(8,128)(2,1)S(1)}, bf16[64,16,128]{2,1,0:T(8,128)(2,1)S(1)}, u32[]{:S(2)}, u32[]{:S(2)}) collective-permute-start(bf16[64,16,128]{2,1,0:T(8,128)(2,1)S(1)} %copy-done.41), channel_id=1, source_target_pairs={{0,12},{4,0},{8,4},{12,8},{1,13},{5,1},{9,5},{13,9},{2,14},{6,2},{... | collective-permute-start | bytes 786440 | tf_op jit(solution)/shard_map/ppermute | solution.py:586
  360.3 24.1 %collective-permute-start.20 = (bf16[64,16,128]{2,1,0:T(8,128)(2,1)}, bf16[64,16,128]{2,1,0:T(8,128)(2,1)S(1)}, u32[]{:S(2)}, u32[]{:S(2)}) collective-permute-start(bf16[64,16,128]{2,1,0:T(8,128)(2,1)} %get-tuple-element.120), channel_id=1, source_target_pairs={{0,4},{4,8},{8,12},{12,0},{1,5},{5,9},{9,13},{13,1},{2,6},{6,10},{... | collective-permute-start | bytes 786440 | tf_op jit(solution)/shard_map/ppermute | solution.py:586
  360.8 33.0 %collective-permute-start.21 = (bf16[64,16,128]{2,1,0:T(8,128)(2,1)}, bf16[64,16,128]{2,1,0:T(8,128)(2,1)S(1)}, u32[]{:S(2)}, u32[]{:S(2)}) collective-permute-start(bf16[64,16,128]{2,1,0:T(8,128)(2,1)} %get-tuple-element.121), channel_id=1, source_target_pairs={{0,8},{4,12},{8,0},{12,4},{1,9},{5,13},{9,1},{13,5},{2,10},{6,14},... | collective-permute-start | bytes 786440 | tf_op jit(solution)/shard_map/ppermute | solution.py:586
  363.1 30.6 %collective-permute-start.22 = (bf16[64,16,128]{2,1,0:T(8,128)(2,1)}, bf16[64,16,128]{2,1,0:T(8,128)(2,1)S(1)}, u32[]{:S(2)}, u32[]{:S(2)}) collective-permute-start(bf16[64,16,128]{2,1,0:T(8,128)(2,1)} %get-tuple-element.122), channel_id=1, source_target_pairs={{0,12},{4,0},{8,4},{12,8},{1,13},{5,1},{9,5},{13,9},{2,14},{6,2},{... | collective-permute-start | bytes 786440 | tf_op jit(solution)/shard_map/ppermute | solution.py:586
  (28 other events, 147.9 us)
where the time goes:
time: 402 us; the launch traced here: 398 us
  Pallas kernels  197 us (49%)
  waiting for transfers between devices  118 us (29%)
  starting transfers between devices  54 us (13%)
  local copies, waits for them, and re-layouts  23.1 us (6%)
    ppermute x32, waiting for transfers between devices, send(): return lax.ppermute(v, 'wide', pairs)  118 us
    pallas_call x6, Pallas kernels, operands(): pl.pallas_call(behind(functools.partial(operand_kernel, sides, first_inde...  61.4 us
    pallas_call x4, Pallas kernels, attention(): pl.pallas_call(functools.partial(attention_kernel, len(pieces)), grid_spe...  54.6 us
    ppermute x32, starting transfers between devices, send(): return lax.ppermute(v, 'wide', pairs)  54 us
    pallas_call x5, Pallas kernels, updates(): pl.pallas_call(behind(update_kernel, 7 + len(small)), grid_spec=pltpu.Pre...  36.8 us
    pallas_call x3, Pallas kernels, products(): pl.pallas_call(behind(functools.partial(product_kernel, members, len(righ...  29.9 us
    pallas_call x4, Pallas kernels, place(): pl.pallas_call(functools.partial(place_kernel, index), grid_spec=pltpu.Pr...  11.4 us
    unnamed x94, local copies, waits for them, and re-layouts  10.1 us
  transfers between devices with their start and end apart: 32, of which 12 were waited for; matrix products, arithmetic and copies ran while one was open for 4% of the time, Pallas kernels for 43%

commit v1 on v0

--- a/solution.py
+++ b/solution.py
@@ -135,9 +135,9 @@
     return pl.BlockSpec(shape, lambda i, s: (0,) * len(shape))
 
 
-def behind(kernel, position):
+def behind(kernel, position, after):
     def run(*refs):
-        kernel(*refs[:position], *refs[position + 1 :])
+        kernel(*refs[:position], *refs[position + len(after) :])
 
     return run
 
@@ -149,14 +149,14 @@
     return
 
 
-def tie(x, after):
+def tie(x, *after):
     return pl.pallas_call(
         nothing,
-        in_specs=[ANYWHERE, ANYWHERE],
+        in_specs=[ANYWHERE] * (1 + len(after)),
         out_specs=ANYWHERE,
         out_shape=jax.ShapeDtypeStruct(x.shape, x.dtype),
         input_output_aliases={0: 0},
-    )(x, after)
+    )(x, *after)
 
 
 def operand_kernel(sides, first_index, slices, scalars, x_ref, gain_ref, weight_ref, *refs):
@@ -191,13 +191,13 @@
             )
 
 
-def operands(x, scalars, first_index, gain, weights, sides, slices, after):
+def operands(x, scalars, first_index, gain, weights, sides, slices, *after):
     rows, count, chan = x.shape
     own = count // 4
     out = jax.ShapeDtypeStruct((chan, rows, count), BF16)
     cut = jax.ShapeDtypeStruct((rows, own, chan), BF16)
     return pl.pallas_call(
-        behind(functools.partial(operand_kernel, sides, first_index, slices), 4),
+        behind(functools.partial(operand_kernel, sides, first_index, slices), 4, after),
         grid_spec=pltpu.PrefetchScalarGridSpec(
             num_scalar_prefetch=1,
             grid=(rows // BLOCK,),
@@ -205,8 +205,8 @@
                 pl.BlockSpec((BLOCK, count, chan), lambda i, s: (i, 0, 0)),
                 full_block(chan, 1),
                 full_block(2 * sides * chan, chan),
-                ANYWHERE,
-            ],
+            ]
+            + [ANYWHERE] * len(after),
             out_specs=[pl.BlockSpec((chan, BLOCK, count), lambda i, s: (0, i, 0))] * sides
             + [pl.BlockSpec((BLOCK, own, chan), lambda i, s: (i, 0, 0))] * len(slices),
             scratch_shapes=[pltpu.VMEM((count // LANES, chan * BLOCK, LANES), F32)] * sides,
@@ -214,7 +214,7 @@
         out_shape=[out] * sides + [cut] * len(slices),
         compiler_params=pltpu.CompilerParams(vmem_limit_bytes=VMEM),
         cost_estimate=COST,
-    )(scalars, x, gain, weights[: 2 * sides * chan], after)
+    )(scalars, x, gain, weights[: 2 * sides * chan], *after)
 
 
 def product_kernel(members, rights, *refs):
@@ -235,7 +235,7 @@
             outs[2 * g + 1][c] = jnp.concatenate([low[:, own:], high[:, own:]], axis=1).astype(BF16)
 
 
-def products(groups, rights, after):
+def products(groups, rights, *after):
     lefts = [v for group in groups for v in group]
     chan, count = lefts[0].shape[0], lefts[0].shape[2]
     rows = [sum(v.shape[1] for v in group) for group in groups]
@@ -246,15 +246,17 @@
     members = [len(group) for group in groups]
     return pl.pallas_call(
         behind(
-            functools.partial(product_kernel, members, len(rights)), len(lefts) + len(rights)
+            functools.partial(product_kernel, members, len(rights)),
+            len(lefts) + len(rights),
+            after,
         ),
         grid=(chan // step,),
-        in_specs=[spec(v) for v in lefts + rights] + [ANYWHERE],
+        in_specs=[spec(v) for v in lefts + rights] + [ANYWHERE] * len(after),
         out_specs=[spec(v) for v in outs],
         out_shape=outs,
         compiler_params=pltpu.CompilerParams(vmem_limit_bytes=VMEM),
         cost_estimate=COST,
-    )(*lefts, *rights, after)
+    )(*lefts, *rights, *after)
 
 
 def update_kernel(
@@ -326,7 +328,7 @@
     bias_ref[...] = bias_work[: heads * BLOCK, :].reshape(heads, BLOCK, wide).astype(BF16)
 
 
-def updates(prod, prod_got, low, high, low_got, high_got, scalars, small, heads, after):
+def updates(prod, prod_got, low, high, low_got, high_got, scalars, small, heads, *after):
     chan, half, wide = prod.shape
     own = wide // 2
 
@@ -340,13 +342,13 @@
     out_spec = pl.BlockSpec((BLOCK, own, chan), lambda i, s: (i, 0, 0))
     pad = small[-1].shape[0]
     return pl.pallas_call(
-        behind(update_kernel, 7 + len(small)),
+        behind(update_kernel, 7 + len(small), after),
         grid_spec=pltpu.PrefetchScalarGridSpec(
             num_scalar_prefetch=1,
             grid=(half // BLOCK,),
             in_specs=[prod_spec, prod_spec, kept(low), kept(high), got(low_got), got(high_got)]
             + [full_block(*v.shape) for v in small]
-            + [ANYWHERE],
+            + [ANYWHERE] * len(after),
             out_specs=[
                 out_spec,
                 out_spec,
@@ -367,57 +369,64 @@
         ],
         compiler_params=pltpu.CompilerParams(vmem_limit_bytes=VMEM),
         cost_estimate=COST,
-    )(scalars, prod, prod_got, low[0], high[0], low_got[0], high_got[0], *small, after)
-
-
-def table_kernel(sizes, scalars, *refs):
-    groups, table = [refs[4 * i : 4 * i + 4] for i in range(len(sizes))], refs[-1]
-    heads, count = table.shape[0], table.shape[1]
+    )(scalars, prod, prod_got, low[0], high[0], low_got[0], high_got[0], *small, *after)
+
+
+def table_kernel(origin, sizes, heads, count, scalars, *refs):
+    group, table = refs[:4], refs[-1]
+    late = len(refs) == 6
     wide = count // 2
     own = wide // 2
     length = scalars[0]
-    for pair in range(2):
-        first = pair * wide
-        for group, members in zip(groups, sizes):
-            start = 0
-            for size in members:
-                half = size // 2
-                for side in range(2):
-                    base = (first + side * half) % count
-                    spot = lax.broadcasted_iota(jnp.int32, (half, wide), 0)
-                    spot = spot + (scalars[3 + base // own] * own + base % own)
-                    masked = jnp.where(spot < length, 0.0, -1e9 * LOG2E)
-                    for h in range(heads):
-                        parts = []
-                        for j in range(2):
-                            source = scalars[16 + 2 * pair + j]
-                            value = group[0][h, start : start + half, :].astype(F32)
-                            for d in range(1, 4):
-                                other = group[d][h, start : start + half, :].astype(F32)
-                                value = jnp.where(source == d, other, value)
-                            parts.append(value[:, side * own : (side + 1) * own])
-                        table[h, base : base + half, pair * wide : (pair + 1) * wide] = (
-                            jnp.concatenate(parts, axis=1) * LOG2E + masked
-                        )
-                start += half
-                first += size
-    return
-
-
-def bias_table(groups, sizes, scalars, heads, count):
-    refs = [v for group in groups for v in group]
+    pairs = [pl.program_id(0)] if late else range(2)
+    for pair in pairs:
+        first, start = origin + pair * wide, 0
+        for size in sizes:
+            half = size // 2
+            for side in range(2):
+                base = (first + side * half) % count
+                spot = lax.broadcasted_iota(jnp.int32, (half, wide), 0)
+                spot = spot + (scalars[3 + base // own] * own + base % own)
+                masked = jnp.where(spot < length, 0.0, -1e9 * LOG2E)
+                for h in range(heads):
+                    parts = []
+                    for j in range(2):
+                        source = scalars[16 + 2 * pair + j]
+                        value = group[0][h, start : start + half, :].astype(F32)
+                        for d in range(1, 4):
+                            other = group[d][h, start : start + half, :].astype(F32)
+                            value = jnp.where(source == d, other, value)
+                        parts.append(value[:, side * own : (side + 1) * own])
+                    value = jnp.concatenate(parts, axis=1) * LOG2E + masked
+                    if late:
+                        table[h, side * half : (side + 1) * half, :] = value
+                    else:
+                        table[h, base : base + half, pair * wide : (pair + 1) * wide] = value
+            start += half
+            first += size
+
+
+def bias_table(group, sizes, origin, table, scalars, heads, count):
+    rest = [] if table is None else [table]
+    size, wide = sizes[0], count // 2
+    block = full_block(heads, count, count)
+    if rest:
+        block = pl.BlockSpec(
+            (heads, size, wide), lambda i, s: (0, (origin + i * wide) % count // size, i)
+        )
     return pl.pallas_call(
-        functools.partial(table_kernel, sizes),
+        functools.partial(table_kernel, origin, sizes, heads, count),
         grid_spec=pltpu.PrefetchScalarGridSpec(
             num_scalar_prefetch=1,
-            grid=(1,),
-            in_specs=[full_block(*v.shape) for v in refs],
-            out_specs=full_block(heads, count, count),
+            grid=(2 if rest else 1,),
+            in_specs=[full_block(*v.shape) for v in group] + [ANYWHERE] * len(rest),
+            out_specs=block,
         ),
         out_shape=jax.ShapeDtypeStruct((heads, count, count), F32),
+        input_output_aliases={5: 0} if rest else {},
         compiler_params=pltpu.CompilerParams(vmem_limit_bytes=VMEM),
         cost_estimate=COST,
-    )(scalars, *refs)
+    )(scalars, *group, *rest)
 
 
 def attention_kernel(parts, scalars, table, gain_ref, w_ref, wo_ref, *refs):
@@ -575,6 +584,7 @@
             jnp.stack([z]),
             jnp.stack([jnp.argmax(order == (z + d) % 4) for d in range(4)]),
             (z - jnp.arange(4)) % 4,
+            jnp.stack([z * own]),
         ]
     ).astype(jnp.int32)
 
@@ -593,14 +603,16 @@
 
     oi_rows = send(own_rows, middle_link)
     p_halves = [send(v, to_inner) for v in (own_rows[:half], own_rows[half:])]
-    left_own, right_own, own_cut, p_got = operands(
-        own_rows, scalars, 8, gain, tri_w, 2, (2, 20), scalars
-    )
+    left_own, right_own, own_cut, p_got = operands(own_rows, scalars, 29, gain, tri_w, 2, (2, 20))
     own_got = send(own_cut, to_outer)
-    p_halves[0] = tie(p_halves[0], left_own)
-    left_pa, right_pa = operands(p_halves[0], scalars, 9, gain, tri_w, 2, (), scalars)
-    p_halves[1] = tie(p_halves[1], left_pa)
-    oo_halves = [send(v, middle_link) for v in p_halves]
+    p_a = tie(p_halves[0], left_own)
+    left_pa, right_pa = operands(p_a, scalars, 9, gain, tri_w, 2, ())
+    oi_rows = tie(oi_rows, left_pa)
+    p_a = tie(p_a, oi_rows)
+    left_oi, oi_cut = operands(oi_rows, scalars, 10, gain, tri_w, 1, (2,))
+    oi_got = send(oi_cut, to_outer)
+    p_b = tie(p_halves[1], left_oi, own_got)
+    oo_halves = [send(v, middle_link) for v in (p_a, p_b)]
 
     bias_w = jnp.zeros((8, chan), BF16).at[:heads].set(att_bias.T)
     small = [
@@ -614,47 +626,44 @@
     near, far = half // BLOCK, half // (2 * BLOCK)
     pieces, biases = [], []
 
-    left_pb, right_pb = operands(p_halves[1], scalars, 13, gain, tri_w, 2, (), left_pa)
+    left_pb, right_pb = operands(p_b, scalars, 13, gain, tri_w, 2, ())
     rights = [right_own, right_pa, right_pb]
-    kept_own, sent_own, kept_p, sent_p = products([[left_own], [left_pa, left_pb]], rights, scalars)
-    left_oi, oi_cut = operands(oi_rows, scalars, 10, gain, tri_w, 1, (2,), kept_p)
-    oi_got = send(oi_cut, to_outer)
-    left_a, a_cut = operands(oo_halves[0], scalars, 11, gain, tri_w, 1, (2,), left_oi)
-    oo_got = [send(a_cut, to_outer)]
-    kept_oi, sent_oi, kept_a, sent_a = products([[left_oi], [left_a]], rights, scalars)
-
-    def update(kept, sent, low, high, low_got, high_got, after):
-        got = send(sent, to_outer)
+    kept_own, sent_own, kept_p, _ = products([[left_own], [left_pa, left_pb]], rights)
+    left_a, a_cut = operands(oo_halves[0], scalars, 11, gain, tri_w, 1, (2,), kept_p, oi_got)
+    a_got = send(a_cut, to_outer)
+    kept_oi, sent_oi, kept_a, sent_a = products([[left_oi], [left_a]], rights)
+
+    def update(kept, got, low, high, low_got, high_got, *after):
         low, high, bias = updates(
-            kept, got, low, high, low_got, high_got, scalars, small, heads, after
+            kept, got, low, high, low_got, high_got, scalars, small, heads, *after
         )
         pieces.extend([low, high])
         biases.append(bias)
         return bias
 
+    def gather(members):
+        joined = members[0] if len(members) == 1 else jnp.concatenate(members, axis=1)
+        return [joined] + [
+            send(joined, [(i, (i + d) % 4) for i in range(4)]) for d in range(1, 4)
+        ]
+
     last = update(
-        kept_own, sent_own, (own_rows, 0), (own_rows, near), (own_got, 0), (own_got, near), kept_oi
-    )
+        kept_own, send(sent_own, to_outer), (own_rows, 0), (own_rows, near), (own_got, 0), (own_got, near), kept_oi
+    )
+    last = update(kept_p, kept_own, (p_a, 0), (p_b, 0), (p_got, 0), (p_got, near), last)
+    left_b, b_cut = operands(oo_halves[1], scalars, 15, gain, tri_w, 1, (2,), last)
+    b_got = send(b_cut, to_outer)
+    kept_b, sent_b = products([[left_b]], rights)
     last = update(
-        kept_p, sent_p, (p_halves[0], 0), (p_halves[1], 0), (p_got, 0), (p_got, near), last
-    )
-    left_b, b_cut = operands(oo_halves[1], scalars, 15, gain, tri_w, 1, (2,), last)
-    oo_got.append(send(b_cut, to_outer))
-    kept_b, sent_b = products([[left_b]], rights, last)
-    last = update(
-        kept_oi, sent_oi, (oi_rows, 0), (oi_rows, near), (oi_got, 0), (oi_got, near), kept_b
-    )
-    for k, (kept, sent) in enumerate(((kept_a, sent_a), (kept_b, sent_b))):
-        low, low_got = oo_halves[k], oo_got[k]
-        last = update(kept, sent, (low, 0), (low, far), (low_got, 0), (low_got, far), last)
-
-    groups, sizes = [], []
-    for members in (biases[:4], biases[4:]):
-        joined = jnp.concatenate(members, axis=1)
-        others = [send(joined, [(i, (i + d) % 4) for i in range(4)]) for d in range(1, 4)]
-        groups.append([joined] + others)
-        sizes.append([2 * v.shape[1] for v in members])
-    table = bias_table(groups, sizes, scalars, heads, count)
+        kept_oi, send(sent_oi, to_outer), (oi_rows, 0), (oi_rows, near), (oi_got, 0), (oi_got, near), kept_b
+    )
+    low = oo_halves[0]
+    last = update(kept_a, send(sent_a, to_outer), (low, 0), (low, far), (a_got, 0), (a_got, far), last)
+    early = [own, own, own, half]
+    table = bias_table(gather(biases), early, 0, None, scalars, heads, count)
+    low = oo_halves[1]
+    last = update(kept_b, send(sent_b, to_outer), (low, 0), (low, far), (b_got, 0), (b_got, far), table)
+    table = bias_table(gather([last]), [half], sum(early), table, scalars, heads, count)
 
     att_w = jnp.swapaxes(att_in, 1, 2).astype(F32) * jnp.array([1, 1, 1, 0.5], F32).reshape(4, 1, 1)
     att_w = att_w.astype(BF16).reshape(4 * chan, chan)

time: 402 us -> 367 us (0.913)
  waiting for transfers between devices: 118 us -> 76.1 us
  starting transfers between devices: 54 us -> 58.8 us
    ppermute x32 -> x31, waiting for transfers between devices: 118 us -> 76.1 us  [send(): return lax.ppermute(v, 'wide', pairs)]
    ppermute x32 -> x31, starting transfers between devices: 54 us -> 58.8 us  [send(): return lax.ppermute(v, 'wide', pairs)]
    pallas_call x8 -> x11, Pallas kernels: 40 us -> 42.2 us  [the longest x5 36.6 us: updates(): pl.pallas_call(behind(update_kernel, 7 + len(small), after), grid_spec=pl...]
  transfers between devices with their start and end apart: 32 -> 31, of which waited for: 12 -> 9; matrix products, arithmetic and copies ran while one was open for 4% -> 5% of each run, Pallas kernels for 43% -> 48%
where the time goes in v1:
time: 367 us; the launch traced here: 363 us
  Pallas kernels  199 us (54%)
  waiting for transfers between devices  76.1 us (21%)
  starting transfers between devices  58.8 us (16%)
  local copies, waits for them, and re-layouts  23.9 us (7%)
  other arithmetic  3.69 us (1%)
    ppermute x31, waiting for transfers between devices, send(): return lax.ppermute(v, 'wide', pairs)  76.1 us
    pallas_call x6, Pallas kernels, operands(): pl.pallas_call(behind(functools.partial(operand_kernel, sides, first_inde...  61.4 us
    ppermute x31, starting transfers between devices, send(): return lax.ppermute(v, 'wide', pairs)  58.8 us
    pallas_call x4, Pallas kernels, attention(): pl.pallas_call(functools.partial(attention_kernel, len(pieces)), grid_spe...  54.6 us
    pallas_call x5, Pallas kernels, updates(): pl.pallas_call(behind(update_kernel, 7 + len(small), after), grid_spec=pl...  36.6 us
    pallas_call x3, Pallas kernels, products(): pl.pallas_call(behind(functools.partial(product_kernel, members, len(righ...  29.8 us
    pallas_call x4, Pallas kernels, place(): pl.pallas_call(functools.partial(place_kernel, index), grid_spec=pltpu.Pr...  11.4 us
    unnamed x94, local copies, waits for them, and re-layouts  10.1 us
  transfers between devices with their start and end apart: 31, of which 9 were waited for; matrix products, arithmetic and copies ran while one was open for 5% of the time, Pallas kernels for 48%

profile of v1, /device:TPU:0, one launch (start us, length us, event | category | flops | bytes accessed | tf_op | source)
XLA Modules:
  0.0 363.2 jit_solution(10844808237629530084)
XLA Ops:
  0.0 2.8 collective-permute-start.1
  2.8 4.8 %slice_bitcast_fusion = (bf16[32,256,128]{2,1,0:T(8,128)(2,1)}, bf16[32,256,128]{2,1,0:T(8,128)(2,1)}) fusion(bf16[1,64,256,128]{3,2,1,0:T(8,128)(2,1)} %param.14), kind=kLoop, calls=%fused_computation | loop fusion | bytes 8388608 | tf_op jit(solution)/shard_map/slice | solution.py:605
  7.6 5.9 %collective-permute-start.2 = (bf16[32,256,128]{2,1,0:T(8,128)(2,1)}, bf16[32,256,128]{2,1,0:T(8,128)(2,1)S(1)}, u32[]{:S(2)}, u32[]{:S(2)}) collective-permute-start(bf16[32,256,128]{2,1,0:T(8,128)(2,1)} %get-tuple-element.135), channel_id=1, source_target_pairs={{0,4},{12,8},{1,5},{13,9},{2,6},{14,10},{3,7},{15,11},{16,20},{28,... | collective-permute-start | bytes 6291464 | tf_op jit(solution)/shard_map/ppermute | solution.py:596
  13.5 2.6 collective-permute-start
  21.3 3.2 concatenate.9.refs_0_.scalars
  24.5 16.3 %shard_map.118 = (bf16[128,64,256]{2,1,0:T(8,128)(2,1)}, bf16[128,64,256]{2,1,0:T(8,128)(2,1)}, bf16[64,64,128]{2,1,0:T(8,128)(2,1)}, bf16[64,64,128]{2,1,0:T(8,128)(2,1)}) custom-call(s32[30]{0:T(128)} %concatenate.9.refs_0_.scalars, bf16[64,256,128]{2,1,0:T(8,128)(2,1)} %bitcast.34, f32[128,1]{1,0:T(8,128)} %copy.22.refs_2_.refs_7_, bf16[512,128]{1,0:T(8,128)(2,1)} %bitcast.41), custom_call_target="tpu_custom_call" | custom-call | flops 1024 | bytes 1024 | tf_op jit(solution)/shard_map/pallas_call | solution.py:199
  42.0 17.7 %collective-permute-done.2.refs_0_ = bf16[32,256,128]{2,1,0:T(8,128)(2,1)S(1)} collective-permute-done((bf16[32,256,128]{2,1,0:T(8,128)(2,1)}, bf16[32,256,128]{2,1,0:T(8,128)(2,1)S(1)}, u32[]{:S(2)}, u32[]{:S(2)}) %collective-permute-start.2) | collective-permute-done | bytes 2097184 | tf_op jit(solution)/shard_map/ppermute | solution.py:596
  61.1 9.7 %shard_map.120 = (bf16[128,32,256]{2,1,0:T(8,128)(2,1)}, bf16[128,32,256]{2,1,0:T(8,128)(2,1)}) custom-call(s32[30]{0:T(128)} %concatenate.9.refs_0_.scalars, bf16[32,256,128]{2,1,0:T(8,128)(2,1)} %shard_map.119.refs_1_.refs_0_, f32[128,1]{1,0:T(8,128)} %copy.22.refs_2_.refs_7_, bf16[512,128]{1,0:T(8,128)(2,1)} %bitcast.42), custom_call_target="tpu_custom_call" | custom-call | flops 1024 | bytes 1024 | tf_op jit(solution)/shard_map/pallas_call | solution.py:199
  70.7 2.0 collective-permute-start.6
  73.4 11.4 %shard_map.122 = (bf16[128,64,256]{2,1,0:T(8,128)(2,1)}, bf16[64,64,128]{2,1,0:T(8,128)(2,1)}) custom-call(s32[30]{0:T(128)} %concatenate.9.refs_0_.scalars, bf16[64,256,128]{2,1,0:T(8,128)(2,1)} %shard_map.121.refs_1_.refs_3_.refs_4_, f32[128,1]{1,0:T(8,128)} %copy.22.refs_2_.refs_7_, bf16[256,128]{1,0:T(8,128)(2,1)} %bitcast.44), custom_call_target="tpu_custom_call" | custom-call | flops 1024 | bytes 1024 | tf_op jit(solution)/shard_map/pallas_call | solution.py:199
  84.8 18.4 %collective-permute-done.refs_0_ = bf16[32,256,128]{2,1,0:T(8,128)(2,1)} collective-permute-done((bf16[32,256,128]{2,1,0:T(8,128)(2,1)}, bf16[32,256,128]{2,1,0:T(8,128)(2,1)}, u32[]{:S(2)}, u32[]{:S(2)}) %collective-permute-start) | collective-permute-done | bytes 2097184 | tf_op jit(solution)/shard_map/ppermute | solution.py:596
  105.3 9.7 %shard_map.124 = (bf16[128,32,256]{2,1,0:T(8,128)(2,1)}, bf16[128,32,256]{2,1,0:T(8,128)(2,1)}) custom-call(s32[30]{0:T(128)} %concatenate.9.refs_0_.scalars, bf16[32,256,128]{2,1,0:T(8,128)(2,1)} %shard_map.123.refs_1_.refs_4_, f32[128,1]{1,0:T(8,128)} %copy.22.refs_2_.refs_7_, bf16[512,128]{1,0:T(8,128)(2,1)} %bitcast.43), custom_call_target="tpu_custom_call" | custom-call | flops 1024 | bytes 1024 | tf_op jit(solution)/shard_map/pallas_call | solution.py:199
  115.0 10.8 %shard_map.125 = (bf16[128,32,128]{2,1,0:T(8,128)(2,1)}, bf16[128,32,128]{2,1,0:T(8,128)(2,1)}, bf16[128,32,128]{2,1,0:T(8,128)(2,1)}, bf16[128,32,128]{2,1,0:T(8,128)(2,1)}) custom-call(bf16[128,64,256]{2,1,0:T(8,128)(2,1)} %get-tuple-element.79.refs_1_.refs_0_, bf16[128,32,256]{2,1,0:T(8,128)(2,1)} %get-tuple-element.80.refs_1_, ...), custom_call_target="tpu_custom_call" | custom-call | flops 1024 | bytes 1024 | tf_op jit(solution)/shard_map/pallas_call | solution.py:247
  127.1 13.4 %collective-permute-done.7.refs_5_.refs_6_ = bf16[64,64,128]{2,1,0:T(8,128)(2,1)S(1)} collective-permute-done((bf16[64,64,128]{2,1,0:T(8,128)(2,1)}, bf16[64,64,128]{2,1,0:T(8,128)(2,1)S(1)}, u32[]{:S(2)}, u32[]{:S(2)}) %collective-permute-start.7) | collective-permute-done | bytes 1048608 | tf_op jit(solution)/shard_map/ppermute | solution.py:596
  141.5 7.1 %shard_map.127 = (bf16[128,32,256]{2,1,0:T(8,128)(2,1)}, bf16[32,64,128]{2,1,0:T(8,128)(2,1)}) custom-call(s32[30]{0:T(128)} %concatenate.9.refs_0_.scalars, bf16[32,256,128]{2,1,0:T(8,128)(2,1)} %collective-permute-done.6.refs_1_.refs_3_.refs_4_, f32[128,1]{1,0:T(8,128)} %copy.22.refs_2_.refs_7_, bf16[256,128]{1,0:T(8,128)(2,1)} %bitcast.45, ...), custom_call_target="tpu_custom_call" | custom-call | flops 1024 | bytes 1024 | tf_op jit(solution)/shard_map/pallas_call | solution.py:199
  148.6 10.1 %shard_map.128 = (bf16[128,32,128]{2,1,0:T(8,128)(2,1)}, bf16[128,32,128]{2,1,0:T(8,128)(2,1)}, bf16[128,16,128]{2,1,0:T(8,128)(2,1)}, bf16[128,16,128]{2,1,0:T(8,128)(2,1)}) custom-call(bf16[128,64,256]{2,1,0:T(8,128)(2,1)} %get-tuple-element.81.refs_1_.refs_0_, bf16[128,32,256]{2,1,0:T(8,128)(2,1)} %get-tuple-element.92.refs_1_, ...), custom_call_target="tpu_custom_call" | custom-call | flops 1024 | bytes 1024 | tf_op jit(solution)/shard_map/pallas_call | solution.py:247
  161.3 1.5 collective-permute-start.12
  165.8 8.5 %shard_map.129 = (bf16[32,64,128]{2,1,0:T(8,128)(2,1)}, bf16[32,64,128]{2,1,0:T(8,128)(2,1)}, bf16[4,32,128]{2,1,0:T(8,128)(2,1)}) custom-call(s32[30]{0:T(128)} %concatenate.9.refs_0_.scalars, bf16[128,32,128]{2,1,0:T(8,128)(2,1)} %get-tuple-element.88.refs_1_.refs_2_, bf16[128,32,128]{2,1,0:T(8,128)(2,1)} %collective-permute-done.5.refs_2_, ...), custom_call_target="tpu_custom_call" | custom-call | flops 1024 | bytes 1024 | tf_op jit(solution)/shard_map/pallas_call | solution.py:344
  174.2 8.5 %shard_map.130 = (bf16[32,64,128]{2,1,0:T(8,128)(2,1)}, bf16[32,64,128]{2,1,0:T(8,128)(2,1)}, bf16[4,32,128]{2,1,0:T(8,128)(2,1)}) custom-call(s32[30]{0:T(128)} %concatenate.9.refs_0_.scalars, bf16[128,32,128]{2,1,0:T(8,128)(2,1)} %get-tuple-element.87.refs_4_.refs_1_, bf16[128,32,128]{2,1,0:T(8,128)(2,1)} %get-tuple-element.88.refs_1_.refs_2_, ...), custom_call_target="tpu_custom_call" | custom-call | flops 1024 | bytes 1024 | tf_op jit(solution)/shard_map/pallas_call | solution.py:344
  184.0 7.3 %shard_map.131 = (bf16[128,32,256]{2,1,0:T(8,128)(2,1)}, bf16[32,64,128]{2,1,0:T(8,128)(2,1)}) custom-call(s32[30]{0:T(128)} %concatenate.9.refs_0_.scalars, bf16[32,256,128]{2,1,0:T(8,128)(2,1)} %copy-done.1, f32[128,1]{1,0:T(8,128)} %copy.22.refs_2_.refs_7_, bf16[256,128]{1,0:T(8,128)(2,1)} %bitcast.46, bf16[4,32,128]{2,1,0:T(8,128)(2,1)} %get-tuple-element.95.refs_4_), custom_call_target="tpu_custom_call" | custom-call | flops 1024 | bytes 1024 | tf_op jit(solution)/shard_map/pallas_call | solution.py:199
  191.3 9.0 %shard_map.132 = (bf16[128,16,128]{2,1,0:T(8,128)(2,1)}, bf16[128,16,128]{2,1,0:T(8,128)(2,1)}) custom-call(bf16[128,32,256]{2,1,0:T(8,128)(2,1)} %get-tuple-element.96.refs_0_, bf16[128,64,256]{2,1,0:T(8,128)(2,1)} %get-tuple-element.84.refs_3_.refs_2_.refs_1_, bf16[128,32,256]{2,1,0:T(8,128)(2,1)} %get-tuple-element.85.refs_4_.refs_3_.refs_2_, ...), custom_call_target="tpu_custom_call" | custom-call | flops 1024 | bytes 1024 | tf_op jit(solution)/shard_map/pallas_call | solution.py:247
  202.9 8.5 %shard_map.133 = (bf16[32,64,128]{2,1,0:T(8,128)(2,1)}, bf16[32,64,128]{2,1,0:T(8,128)(2,1)}, bf16[4,32,128]{2,1,0:T(8,128)(2,1)}) custom-call(s32[30]{0:T(128)} %concatenate.9.refs_0_.scalars, bf16[128,32,128]{2,1,0:T(8,128)(2,1)} %get-tuple-element.93.refs_13_.refs_1_, bf16[128,32,128]{2,1,0:T(8,128)(2,1)} %collective-permute-done.10.refs_2_, ...), custom_call_target="tpu_custom_call" | custom-call | flops 1024 | bytes 1024 | tf_op jit(solution)/shard_map/pallas_call | solution.py:344
  212.4 5.7 %shard_map.134 = (bf16[16,64,128]{2,1,0:T(8,128)(2,1)}, bf16[16,64,128]{2,1,0:T(8,128)(2,1)}, bf16[4,16,128]{2,1,0:T(8,128)(2,1)}) custom-call(s32[30]{0:T(128)} %concatenate.9.refs_0_.scalars, bf16[128,16,128]{2,1,0:T(8,128)(2,1)} %get-tuple-element.102.refs_1_, bf16[128,16,128]{2,1,0:T(8,128)(2,1)} %copy-done.6, ...), custom_call_target="tpu_custom_call" | custom-call | flops 1024 | bytes 1024 | tf_op jit(solution)/shard_map/pallas_call | solution.py:344
  218.8 8.5 %collective-permute-start.13 = (bf16[4,112,128]{2,1,0:T(8,128)(2,1)S(1)}, bf16[4,112,128]{2,1,0:T(8,128)(2,1)S(1)}, u32[]{:S(2)}, u32[]{:S(2)}) collective-permute-start(bf16[4,112,128]{2,1,0:T(8,128)(2,1)S(1)} %constant_dynamic-update-slice_fusion.refs_0_), channel_id=1, source_target_pairs={{0,4},{4,8},{8,12},{12,0},{1,5},{5,9},{9,13},{13,1},{2,6},{6,10},{... | collective-permute-start | bytes 344072 | tf_op jit(solution)/shard_map/ppermute | solution.py:596
  228.4 2.9 collective-permute-start.15
  231.3 3.6 collective-permute-done.14.refs_2_
  234.9 4.1 %collective-permute-done.15.refs_3_ = bf16[4,112,128]{2,1,0:T(8,128)(2,1)S(1)} collective-permute-done((bf16[4,112,128]{2,1,0:T(8,128)(2,1)S(1)}, bf16[4,112,128]{2,1,0:T(8,128)(2,1)S(1)}, u32[]{:S(2)}, u32[]{:S(2)}) %collective-permute-start.15) | collective-permute-done | bytes 114720 | tf_op jit(solution)/shard_map/ppermute | solution.py:596
  239.6 3.2 shard_map.135.refs_13_.refs_4_
  244.4 5.5 %shard_map.136 = (bf16[16,64,128]{2,1,0:T(8,128)(2,1)}, bf16[16,64,128]{2,1,0:T(8,128)(2,1)}, bf16[4,16,128]{2,1,0:T(8,128)(2,1)}) custom-call(s32[30]{0:T(128)} %concatenate.9.refs_0_.scalars, bf16[128,16,128]{2,1,0:T(8,128)(2,1)} %get-tuple-element.97.refs_13_.refs_1_, bf16[128,16,128]{2,1,0:T(8,128)(2,1)} %copy-done.7, bf16[32,256,128]{2,1,0:T(8,128)(2,1)} %copy-done.1, ...), custom_call_target="tpu_custom_call" | custom-call | flops 1024 | bytes 1024 | tf_op jit(solution)/shard_map/pallas_call | solution.py:344
  250.0 3.7 %collective-permute-start.17 = (bf16[4,16,128]{2,1,0:T(8,128)(2,1)}, bf16[4,16,128]{2,1,0:T(8,128)(2,1)S(1)}, u32[]{:S(2)}, u32[]{:S(2)}) collective-permute-start(bf16[4,16,128]{2,1,0:T(8,128)(2,1)} %get-tuple-element.106.refs_0_), channel_id=1, source_target_pairs={{0,8},{4,12},{8,0},{12,4},{1,9},{5,13},{9,1},{13,5},{2,10},{6,14},... | collective-permute-start | bytes 49160 | tf_op jit(solution)/shard_map/ppermute | solution.py:596
  255.8 1.8 collective-permute-done.18.refs_3_
  258.3 2.4 shard_map.137.table
  260.7 13.6 %shard_map.141 = (bf16[64,16,128]{2,1,0:T(8,128)(2,1)}, bf16[64,16,128]{2,1,0:T(8,128)(2,1)}, bf16[64,16,128]{2,1,0:T(8,128)(2,1)}, bf16[64,16,128]{2,1,0:T(8,128)(2,1)}) custom-call(s32[30]{0:T(128)} %concatenate.9.refs_0_.scalars, f32[4,256,256]{2,1,0:T(8,128)} %shard_map.137.table, f32[128,1]{1,0:T(8,128)} %copy.35.refs_9_.gain_ref, ...), custom_call_target="tpu_custom_call" | custom-call | flops 1024 | bytes 1024 | tf_op jit(solution)/shard_map/pallas_call | solution.py:501
  274.9 2.2 collective-permute-start.29
  277.1 1.6 collective-permute-start.30
  278.7 13.6 %shard_map.140 = (bf16[64,16,128]{2,1,0:T(8,128)(2,1)}, bf16[64,16,128]{2,1,0:T(8,128)(2,1)}, bf16[64,16,128]{2,1,0:T(8,128)(2,1)}, bf16[64,16,128]{2,1,0:T(8,128)(2,1)}) custom-call(s32[30]{0:T(128)} %concatenate.9.refs_0_.scalars, f32[4,256,256]{2,1,0:T(8,128)} %shard_map.137.table, f32[128,1]{1,0:T(8,128)} %copy.35.refs_9_.gain_ref, ...), custom_call_target="tpu_custom_call" | custom-call | flops 1024 | bytes 1024 | tf_op jit(solution)/shard_map/pallas_call | solution.py:501
  293.8 13.6 %shard_map.139 = (bf16[64,16,128]{2,1,0:T(8,128)(2,1)}, bf16[64,16,128]{2,1,0:T(8,128)(2,1)}, bf16[64,16,128]{2,1,0:T(8,128)(2,1)}, bf16[64,16,128]{2,1,0:T(8,128)(2,1)}) custom-call(s32[30]{0:T(128)} %concatenate.9.refs_0_.scalars, f32[4,256,256]{2,1,0:T(8,128)} %shard_map.137.table, f32[128,1]{1,0:T(8,128)} %copy.35.refs_9_.gain_ref, ...), custom_call_target="tpu_custom_call" | custom-call | flops 1024 | bytes 1024 | tf_op jit(solution)/shard_map/pallas_call | solution.py:501
  307.5 2.9 collective-permute-start.27
  310.5 13.8 %shard_map.138 = (bf16[64,16,128]{2,1,0:T(8,128)(2,1)}, bf16[64,16,128]{2,1,0:T(8,128)(2,1)}, bf16[64,16,128]{2,1,0:T(8,128)(2,1)}, bf16[64,16,128]{2,1,0:T(8,128)(2,1)}) custom-call(s32[30]{0:T(128)} %concatenate.9.refs_0_.scalars, f32[4,256,256]{2,1,0:T(8,128)} %shard_map.137.table, f32[128,1]{1,0:T(8,128)} %copy.35.refs_9_.gain_ref, ...), custom_call_target="tpu_custom_call" | custom-call | flops 1024 | bytes 1024 | tf_op jit(solution)/shard_map/pallas_call | solution.py:501
  324.3 1.5 collective-permute-start.23
  325.8 2.8 collective-permute-start.24
  330.2 2.8 collective-permute-start.21
  333.0 2.8 shard_map.142.refs_4_
  335.9 2.8 shard_map.143.refs_4_
  338.8 9.4 %collective-permute-done.23.refs_2_ = bf16[64,16,128]{2,1,0:T(8,128)(2,1)S(1)} collective-permute-done((bf16[64,16,128]{2,1,0:T(8,128)(2,1)S(1)}, bf16[64,16,128]{2,1,0:T(8,128)(2,1)S(1)}, u32[]{:S(2)}, u32[]{:S(2)}) %collective-permute-start.23) | collective-permute-done | bytes 262176 | tf_op jit(solution)/shard_map/ppermute | solution.py:596
  349.0 2.8 shard_map.144.refs_4_
  351.8 7.6 %collective-permute-done.20.refs_2_ = bf16[64,16,128]{2,1,0:T(8,128)(2,1)S(1)} collective-permute-done((bf16[64,16,128]{2,1,0:T(8,128)(2,1)}, bf16[64,16,128]{2,1,0:T(8,128)(2,1)S(1)}, u32[]{:S(2)}, u32[]{:S(2)}) %collective-permute-start.20) | collective-permute-done | bytes 262176 | tf_op jit(solution)/shard_map/ppermute | solution.py:596
  360.2 2.8 shard_map.145
  (157 shorter events, 34.8 us)
Async XLA Ops:
  0.0 16.2 %copy-start.24 = (bf16[4,128,128]{2,1,0:T(8,128)(2,1)S(1)}, bf16[4,128,128]{2,1,0:T(8,128)(2,1)}, u32[]{:S(2)}) copy-start(bf16[4,128,128]{2,1,0:T(8,128)(2,1)} %param.17) | copy-start | bytes 393220
  0.0 16.9 %copy-start.36 = (f32[128]{0:T(128)S(1)}, f32[128]{0:T(128)}, u32[]{:S(2)}) copy-start(f32[128]{0:T(128)} %param.16) | copy-start | bytes 1540
  0.0 70.7 %collective-permute-start.1 = (bf16[64,256,128]{2,1,0:T(8,128)(2,1)}, bf16[64,256,128]{2,1,0:T(8,128)(2,1)}, u32[]{:S(2)}, u32[]{:S(2)}) collective-permute-start(bf16[64,256,128]{2,1,0:T(8,128)(2,1)} %bitcast.33), channel_id=1, source_target_pairs={{4,8},{8,4},{5,9},{9,5},{6,10},{10,6},{7,11},{11,7},{20,24},{24,20... | collective-permute-start | bytes 12582920 | tf_op jit(solution)/shard_map/ppermute | solution.py:596
  7.6 52.1 %collective-permute-start.2 = (bf16[32,256,128]{2,1,0:T(8,128)(2,1)}, bf16[32,256,128]{2,1,0:T(8,128)(2,1)S(1)}, u32[]{:S(2)}, u32[]{:S(2)}) collective-permute-start(bf16[32,256,128]{2,1,0:T(8,128)(2,1)} %get-tuple-element.135), channel_id=1, source_target_pairs={{0,4},{12,8},{1,5},{13,9},{2,6},{14,10},{3,7},{15,11},{16,20},{28,... | collective-permute-start | bytes 6291464 | tf_op jit(solution)/shard_map/ppermute | solution.py:596
  13.5 89.7 %collective-permute-start = (bf16[32,256,128]{2,1,0:T(8,128)(2,1)}, bf16[32,256,128]{2,1,0:T(8,128)(2,1)}, u32[]{:S(2)}, u32[]{:S(2)}) collective-permute-start(bf16[32,256,128]{2,1,0:T(8,128)(2,1)} %get-tuple-element.136), channel_id=1, source_target_pairs={{0,4},{12,8},{1,5},{13,9},{2,6},{14,10},{3,7},{15,11},{16,20},{28,... | collective-permute-start | bytes 6291464 | tf_op jit(solution)/shard_map/ppermute | solution.py:596
  40.8 44.1 %collective-permute-start.3 = (bf16[64,64,128]{2,1,0:T(8,128)(2,1)}, bf16[64,64,128]{2,1,0:T(8,128)(2,1)S(1)}, u32[]{:S(2)}, u32[]{:S(2)}) collective-permute-start(bf16[64,64,128]{2,1,0:T(8,128)(2,1)} %get-tuple-element.82), channel_id=1, source_target_pairs={{4,0},{8,12},{5,1},{9,13},{6,2},{10,14},{7,3},{11,15},{20,16},{24,... | collective-permute-start | bytes 3145736 | tf_op jit(solution)/shard_map/ppermute | solution.py:596
  70.7 69.8 %collective-permute-start.6 = (bf16[32,256,128]{2,1,0:T(8,128)(2,1)}, bf16[32,256,128]{2,1,0:T(8,128)(2,1)}, u32[]{:S(2)}, u32[]{:S(2)}) collective-permute-start(bf16[32,256,128]{2,1,0:T(8,128)(2,1)} %shard_map.126.refs_3_), channel_id=1, source_target_pairs={{4,8},{8,4},{5,9},{9,5},{6,10},{10,6},{7,11},{11,7},{20,24},{24,20... | collective-permute-start | bytes 6291464 | tf_op jit(solution)/shard_map/ppermute | solution.py:596
  84.8 18.4 %copy-start.3 = (bf16[64,64,128]{2,1,0:T(8,128)(2,1)}, bf16[64,64,128]{2,1,0:T(8,128)(2,1)S(1)}, u32[]{:S(2)}) copy-start(bf16[64,64,128]{2,1,0:T(8,128)(2,1)S(1)} %collective-permute-done.3.refs_2_.refs_5_.refs_6_) | copy-start | bytes 3145732
  103.2 79.5 %collective-permute-start.4 = (bf16[32,256,128]{2,1,0:T(8,128)(2,1)}, bf16[32,256,128]{2,1,0:T(8,128)(2,1)S(1)}, u32[]{:S(2)}, u32[]{:S(2)}) collective-permute-start(bf16[32,256,128]{2,1,0:T(8,128)(2,1)} %shard_map.123.refs_1_.refs_4_), channel_id=1, source_target_pairs={{4,8},{8,4},{5,9},{9,5},{6,10},{10,6},{7,11},{11,7},{20,24},{24,20... | collective-permute-start | bytes 6291464 | tf_op jit(solution)/shard_map/ppermute | solution.py:596
  104.0 36.5 %collective-permute-start.7 = (bf16[64,64,128]{2,1,0:T(8,128)(2,1)}, bf16[64,64,128]{2,1,0:T(8,128)(2,1)S(1)}, u32[]{:S(2)}, u32[]{:S(2)}) collective-permute-start(bf16[64,64,128]{2,1,0:T(8,128)(2,1)} %get-tuple-element.91), channel_id=1, source_target_pairs={{4,0},{8,12},{5,1},{9,13},{6,2},{10,14},{7,3},{11,15},{20,16},{24,... | collective-permute-start | bytes 3145736 | tf_op jit(solution)/shard_map/ppermute | solution.py:596
  125.8 40.0 %collective-permute-start.5 = (bf16[128,32,128]{2,1,0:T(8,128)(2,1)}, bf16[128,32,128]{2,1,0:T(8,128)(2,1)}, u32[]{:S(2)}, u32[]{:S(2)}) collective-permute-start(bf16[128,32,128]{2,1,0:T(8,128)(2,1)} %get-tuple-element.90), channel_id=1, source_target_pairs={{4,0},{8,12},{5,1},{9,13},{6,2},{10,14},{7,3},{11,15},{20,16},{24,... | collective-permute-start | bytes 3145736 | tf_op jit(solution)/shard_map/ppermute | solution.py:596
  148.6 14.2 %copy-start.37 = (f32[128]{0:T(128)S(1)}, f32[128]{0:T(128)}, u32[]{:S(2)}) copy-start(f32[128]{0:T(128)} %param.21) | copy-start | bytes 1540
  148.6 15.0 %copy-start.29 = (bf16[128,128]{1,0:T(8,128)(2,1)S(1)}, bf16[128,128]{1,0:T(8,128)(2,1)}, u32[]{:S(2)}) copy-start(bf16[128,128]{1,0:T(8,128)(2,1)} %param.20) | copy-start | bytes 98308
  148.6 15.1 %copy-start.30 = (bf16[128,128]{1,0:T(8,128)(2,1)S(1)}, bf16[128,128]{1,0:T(8,128)(2,1)}, u32[]{:S(2)}) copy-start(bf16[128,128]{1,0:T(8,128)(2,1)} %param.18) | copy-start | bytes 98308
  148.6 15.2 %copy-start.38 = (f32[128]{0:T(128)S(1)}, f32[128]{0:T(128)}, u32[]{:S(2)}) copy-start(f32[128]{0:T(128)} %param.19) | copy-start | bytes 1540
  148.6 15.9 %copy-start.35 = (bf16[128,4]{0,1:T(4,128)(2,1)S(1)}, bf16[128,4]{0,1:T(4,128)(2,1)}, u32[]{:S(2)}) copy-start(bf16[128,4]{0,1:T(4,128)(2,1)} %param.23) | copy-start | bytes 3076
  158.7 44.2 %collective-permute-start.10 = (bf16[128,32,128]{2,1,0:T(8,128)(2,1)}, bf16[128,32,128]{2,1,0:T(8,128)(2,1)}, u32[]{:S(2)}, u32[]{:S(2)}) collective-permute-start(bf16[128,32,128]{2,1,0:T(8,128)(2,1)} %get-tuple-element.100), channel_id=1, source_target_pairs={{4,0},{8,12},{5,1},{9,13},{6,2},{10,14},{7,3},{11,15},{20,16},{24,... | collective-permute-start | bytes 3145736 | tf_op jit(solution)/shard_map/ppermute | solution.py:596
  160.0 51.4 %collective-permute-start.11 = (bf16[128,16,128]{2,1,0:T(8,128)(2,1)}, bf16[128,16,128]{2,1,0:T(8,128)(2,1)S(1)}, u32[]{:S(2)}, u32[]{:S(2)}) collective-permute-start(bf16[128,16,128]{2,1,0:T(8,128)(2,1)} %get-tuple-element.103), channel_id=1, source_target_pairs={{4,0},{8,12},{5,1},{9,13},{6,2},{10,14},{7,3},{11,15},{20,16},{24,... | collective-permute-start | bytes 1572872 | tf_op jit(solution)/shard_map/ppermute | solution.py:596
  161.3 50.1 %collective-permute-start.12 = (bf16[32,64,128]{2,1,0:T(8,128)(2,1)}, bf16[32,64,128]{2,1,0:T(8,128)(2,1)S(1)}, u32[]{:S(2)}, u32[]{:S(2)}) collective-permute-start(bf16[32,64,128]{2,1,0:T(8,128)(2,1)} %get-tuple-element.104), channel_id=1, source_target_pairs={{4,0},{8,12},{5,1},{9,13},{6,2},{10,14},{7,3},{11,15},{20,16},{24,... | collective-permute-start | bytes 1572872 | tf_op jit(solution)/shard_map/ppermute | solution.py:596
  191.3 11.6 %copy-start.21 = (bf16[4,32,128]{2,1,0:T(8,128)(2,1)S(1)}, bf16[4,32,128]{2,1,0:T(8,128)(2,1)}, u32[]{:S(2)}) copy-start(bf16[4,32,128]{2,1,0:T(8,128)(2,1)} %get-tuple-element.94.refs_13_) | copy-start | bytes 98308
  191.3 11.6 %copy-start.22 = (bf16[4,32,128]{2,1,0:T(8,128)(2,1)S(1)}, bf16[4,32,128]{2,1,0:T(8,128)(2,1)}, u32[]{:S(2)}) copy-start(bf16[4,32,128]{2,1,0:T(8,128)(2,1)} %get-tuple-element.95.refs_4_) | copy-start | bytes 98308
  200.3 42.5 %collective-permute-start.8 = (bf16[128,16,128]{2,1,0:T(8,128)(2,1)}, bf16[128,16,128]{2,1,0:T(8,128)(2,1)S(1)}, u32[]{:S(2)}, u32[]{:S(2)}) collective-permute-start(bf16[128,16,128]{2,1,0:T(8,128)(2,1)} %get-tuple-element.98), channel_id=1, source_target_pairs={{4,0},{8,12},{5,1},{9,13},{6,2},{10,14},{7,3},{11,15},{20,16},{24,... | collective-permute-start | bytes 1572872 | tf_op jit(solution)/shard_map/ppermute | solution.py:596
  201.6 41.2 %collective-permute-start.9 = (bf16[32,64,128]{2,1,0:T(8,128)(2,1)S(1)}, bf16[32,64,128]{2,1,0:T(8,128)(2,1)S(1)}, u32[]{:S(2)}, u32[]{:S(2)}) collective-permute-start(bf16[32,64,128]{2,1,0:T(8,128)(2,1)S(1)} %copy-done.40), channel_id=1, source_target_pairs={{4,0},{8,12},{5,1},{9,13},{6,2},{10,14},{7,3},{11,15},{20,16},{24,... | collective-permute-start | bytes 1572872 | tf_op jit(solution)/shard_map/ppermute | solution.py:596
  218.8 20.1 %copy-start.20 = (bf16[4,112,128]{2,1,0:T(8,128)(2,1)}, bf16[4,112,128]{2,1,0:T(8,128)(2,1)S(1)}, u32[]{:S(2)}) copy-start(bf16[4,112,128]{2,1,0:T(8,128)(2,1)S(1)} %constant_dynamic-update-slice_fusion.refs_0_) | copy-start | bytes 344068
  218.8 12.5 %collective-permute-start.13 = (bf16[4,112,128]{2,1,0:T(8,128)(2,1)S(1)}, bf16[4,112,128]{2,1,0:T(8,128)(2,1)S(1)}, u32[]{:S(2)}, u32[]{:S(2)}) collective-permute-start(bf16[4,112,128]{2,1,0:T(8,128)(2,1)S(1)} %constant_dynamic-update-slice_fusion.refs_0_), channel_id=1, source_target_pairs={{0,4},{4,8},{8,12},{12,0},{1,5},{5,9},{9,13},{13,1},{2,6},{6,10},{... | collective-permute-start | bytes 344072 | tf_op jit(solution)/shard_map/ppermute | solution.py:596
  227.3 7.6 %collective-permute-start.14 = (bf16[4,112,128]{2,1,0:T(8,128)(2,1)S(1)}, bf16[4,112,128]{2,1,0:T(8,128)(2,1)S(1)}, u32[]{:S(2)}, u32[]{:S(2)}) collective-permute-start(bf16[4,112,128]{2,1,0:T(8,128)(2,1)S(1)} %constant_dynamic-update-slice_fusion.refs_0_), channel_id=1, source_target_pairs={{0,8},{4,12},{8,0},{12,4},{1,9},{5,13},{9,1},{13,5},{2,10},{6,14},... | collective-permute-start | bytes 344072 | tf_op jit(solution)/shard_map/ppermute | solution.py:596
  228.4 10.6 %collective-permute-start.15 = (bf16[4,112,128]{2,1,0:T(8,128)(2,1)S(1)}, bf16[4,112,128]{2,1,0:T(8,128)(2,1)S(1)}, u32[]{:S(2)}, u32[]{:S(2)}) collective-permute-start(bf16[4,112,128]{2,1,0:T(8,128)(2,1)S(1)} %constant_dynamic-update-slice_fusion.refs_0_), channel_id=1, source_target_pairs={{0,12},{4,0},{8,4},{12,8},{1,13},{5,1},{9,5},{13,9},{2,14},{6,2},{... | collective-permute-start | bytes 344072 | tf_op jit(solution)/shard_map/ppermute | solution.py:596
  242.8 12.2 %copy-start.31 = (bf16[128,128]{1,0:T(8,128)(2,1)S(1)}, bf16[128,128]{1,0:T(8,128)(2,1)}, u32[]{:S(2)}) copy-start(bf16[128,128]{1,0:T(8,128)(2,1)} %param.24) | copy-start | bytes 98308
  250.0 5.8 %collective-permute-start.16 = (bf16[4,16,128]{2,1,0:T(8,128)(2,1)}, bf16[4,16,128]{2,1,0:T(8,128)(2,1)S(1)}, u32[]{:S(2)}, u32[]{:S(2)}) collective-permute-start(bf16[4,16,128]{2,1,0:T(8,128)(2,1)} %get-tuple-element.106.refs_0_), channel_id=1, source_target_pairs={{0,4},{4,8},{8,12},{12,0},{1,5},{5,9},{9,13},{13,1},{2,6},{6,10},{... | collective-permute-start | bytes 49160 | tf_op jit(solution)/shard_map/ppermute | solution.py:596
  250.0 5.9 %collective-permute-start.17 = (bf16[4,16,128]{2,1,0:T(8,128)(2,1)}, bf16[4,16,128]{2,1,0:T(8,128)(2,1)S(1)}, u32[]{:S(2)}, u32[]{:S(2)}) collective-permute-start(bf16[4,16,128]{2,1,0:T(8,128)(2,1)} %get-tuple-element.106.refs_0_), channel_id=1, source_target_pairs={{0,8},{4,12},{8,0},{12,4},{1,9},{5,13},{9,1},{13,5},{2,10},{6,14},... | collective-permute-start | bytes 49160 | tf_op jit(solution)/shard_map/ppermute | solution.py:596
  253.7 3.9 %collective-permute-start.18 = (bf16[4,16,128]{2,1,0:T(8,128)(2,1)}, bf16[4,16,128]{2,1,0:T(8,128)(2,1)S(1)}, u32[]{:S(2)}, u32[]{:S(2)}) collective-permute-start(bf16[4,16,128]{2,1,0:T(8,128)(2,1)} %get-tuple-element.106.refs_0_), channel_id=1, source_target_pairs={{0,12},{4,0},{8,4},{12,8},{1,13},{5,1},{9,5},{13,9},{2,14},{6,2},{... | collective-permute-start | bytes 49160 | tf_op jit(solution)/shard_map/ppermute | solution.py:596
  274.3 33.2 %collective-permute-start.28 = (bf16[64,16,128]{2,1,0:T(8,128)(2,1)}, bf16[64,16,128]{2,1,0:T(8,128)(2,1)S(1)}, u32[]{:S(2)}, u32[]{:S(2)}) collective-permute-start(bf16[64,16,128]{2,1,0:T(8,128)(2,1)} %get-tuple-element.130), channel_id=1, source_target_pairs={{0,4},{4,8},{8,12},{12,0},{1,5},{5,9},{9,13},{13,1},{2,6},{6,10},{... | collective-permute-start | bytes 786440 | tf_op jit(solution)/shard_map/ppermute | solution.py:596
  274.9 35.4 %collective-permute-start.29 = (bf16[64,16,128]{2,1,0:T(8,128)(2,1)}, bf16[64,16,128]{2,1,0:T(8,128)(2,1)S(1)}, u32[]{:S(2)}, u32[]{:S(2)}) collective-permute-start(bf16[64,16,128]{2,1,0:T(8,128)(2,1)} %get-tuple-element.131), channel_id=1, source_target_pairs={{0,8},{4,12},{8,0},{12,4},{1,9},{5,13},{9,1},{13,5},{2,10},{6,14},... | collective-permute-start | bytes 786440 | tf_op jit(solution)/shard_map/ppermute | solution.py:596
  277.1 47.2 %collective-permute-start.30 = (bf16[64,16,128]{2,1,0:T(8,128)(2,1)}, bf16[64,16,128]{2,1,0:T(8,128)(2,1)S(1)}, u32[]{:S(2)}, u32[]{:S(2)}) collective-permute-start(bf16[64,16,128]{2,1,0:T(8,128)(2,1)} %get-tuple-element.132), channel_id=1, source_target_pairs={{0,12},{4,0},{8,4},{12,8},{1,13},{5,1},{9,5},{13,9},{2,14},{6,2},{... | collective-permute-start | bytes 786440 | tf_op jit(solution)/shard_map/ppermute | solution.py:596
  292.3 33.5 %collective-permute-start.25 = (bf16[64,16,128]{2,1,0:T(8,128)(2,1)}, bf16[64,16,128]{2,1,0:T(8,128)(2,1)S(1)}, u32[]{:S(2)}, u32[]{:S(2)}) collective-permute-start(bf16[64,16,128]{2,1,0:T(8,128)(2,1)} %get-tuple-element.126), channel_id=1, source_target_pairs={{0,4},{4,8},{8,12},{12,0},{1,5},{5,9},{9,13},{13,1},{2,6},{6,10},{... | collective-permute-start | bytes 786440 | tf_op jit(solution)/shard_map/ppermute | solution.py:596
  292.7 14.7 %copy-start.43 = (bf16[64,16,128]{2,1,0:T(8,128)(2,1)S(1)}, bf16[64,16,128]{2,1,0:T(8,128)(2,1)}, u32[]{:S(2)}) copy-start(bf16[64,16,128]{2,1,0:T(8,128)(2,1)} %get-tuple-element.128) | copy-start | bytes 786436
  292.7 35.9 %collective-permute-start.26 = (bf16[64,16,128]{2,1,0:T(8,128)(2,1)}, bf16[64,16,128]{2,1,0:T(8,128)(2,1)S(1)}, u32[]{:S(2)}, u32[]{:S(2)}) collective-permute-start(bf16[64,16,128]{2,1,0:T(8,128)(2,1)} %get-tuple-element.127), channel_id=1, source_target_pairs={{0,8},{4,12},{8,0},{12,4},{1,9},{5,13},{9,1},{13,5},{2,10},{6,14},... | collective-permute-start | bytes 786440 | tf_op jit(solution)/shard_map/ppermute | solution.py:596
  307.4 16.8 %copy-start.17 = (bf16[64,16,128]{2,1,0:T(8,128)(2,1)}, bf16[64,16,128]{2,1,0:T(8,128)(2,1)S(1)}, u32[]{:S(2)}) copy-start(bf16[64,16,128]{2,1,0:T(8,128)(2,1)S(1)} %collective-permute-done.28.refs_1_) | copy-start | bytes 786436
  307.5 21.3 %collective-permute-start.27 = (bf16[64,16,128]{2,1,0:T(8,128)(2,1)S(1)}, bf16[64,16,128]{2,1,0:T(8,128)(2,1)S(1)}, u32[]{:S(2)}, u32[]{:S(2)}) collective-permute-start(bf16[64,16,128]{2,1,0:T(8,128)(2,1)S(1)} %copy-done.43), channel_id=1, source_target_pairs={{0,12},{4,0},{8,4},{12,8},{1,13},{5,1},{9,5},{13,9},{2,14},{6,2},{... | collective-permute-start | bytes 786440 | tf_op jit(solution)/shard_map/ppermute | solution.py:596
  310.3 13.9 %copy-start.18 = (bf16[64,16,128]{2,1,0:T(8,128)(2,1)}, bf16[64,16,128]{2,1,0:T(8,128)(2,1)S(1)}, u32[]{:S(2)}) copy-start(bf16[64,16,128]{2,1,0:T(8,128)(2,1)S(1)} %collective-permute-done.29.refs_2_) | copy-start | bytes 786436
  310.4 14.0 %copy-start.42 = (bf16[64,16,128]{2,1,0:T(8,128)(2,1)S(1)}, bf16[64,16,128]{2,1,0:T(8,128)(2,1)}, u32[]{:S(2)}) copy-start(bf16[64,16,128]{2,1,0:T(8,128)(2,1)} %get-tuple-element.123) | copy-start | bytes 786436
  310.4 15.5 %copy-start.41 = (bf16[64,16,128]{2,1,0:T(8,128)(2,1)S(1)}, bf16[64,16,128]{2,1,0:T(8,128)(2,1)}, u32[]{:S(2)}) copy-start(bf16[64,16,128]{2,1,0:T(8,128)(2,1)} %get-tuple-element.124) | copy-start | bytes 786436
  310.4 19.8 %collective-permute-start.22 = (bf16[64,16,128]{2,1,0:T(8,128)(2,1)}, bf16[64,16,128]{2,1,0:T(8,128)(2,1)S(1)}, u32[]{:S(2)}, u32[]{:S(2)}) collective-permute-start(bf16[64,16,128]{2,1,0:T(8,128)(2,1)} %get-tuple-element.122), channel_id=1, source_target_pairs={{0,4},{4,8},{8,12},{12,0},{1,5},{5,9},{9,13},{13,1},{2,6},{6,10},{... | collective-permute-start | bytes 786440 | tf_op jit(solution)/shard_map/ppermute | solution.py:596
  324.3 23.8 %collective-permute-start.23 = (bf16[64,16,128]{2,1,0:T(8,128)(2,1)S(1)}, bf16[64,16,128]{2,1,0:T(8,128)(2,1)S(1)}, u32[]{:S(2)}, u32[]{:S(2)}) collective-permute-start(bf16[64,16,128]{2,1,0:T(8,128)(2,1)S(1)} %copy-done.42), channel_id=1, source_target_pairs={{0,8},{4,12},{8,0},{12,4},{1,9},{5,13},{9,1},{13,5},{2,10},{6,14},... | collective-permute-start | bytes 786440 | tf_op jit(solution)/shard_map/ppermute | solution.py:596
  325.8 22.3 %collective-permute-start.24 = (bf16[64,16,128]{2,1,0:T(8,128)(2,1)S(1)}, bf16[64,16,128]{2,1,0:T(8,128)(2,1)S(1)}, u32[]{:S(2)}, u32[]{:S(2)}) collective-permute-start(bf16[64,16,128]{2,1,0:T(8,128)(2,1)S(1)} %copy-done.41), channel_id=1, source_target_pairs={{0,12},{4,0},{8,4},{12,8},{1,13},{5,1},{9,5},{13,9},{2,14},{6,2},{... | collective-permute-start | bytes 786440 | tf_op jit(solution)/shard_map/ppermute | solution.py:596
  328.7 23.1 %collective-permute-start.19 = (bf16[64,16,128]{2,1,0:T(8,128)(2,1)}, bf16[64,16,128]{2,1,0:T(8,128)(2,1)S(1)}, u32[]{:S(2)}, u32[]{:S(2)}) collective-permute-start(bf16[64,16,128]{2,1,0:T(8,128)(2,1)} %get-tuple-element.118), channel_id=1, source_target_pairs={{0,4},{4,8},{8,12},{12,0},{1,5},{5,9},{9,13},{13,1},{2,6},{6,10},{... | collective-permute-start | bytes 786440 | tf_op jit(solution)/shard_map/ppermute | solution.py:596
  328.7 30.7 %collective-permute-start.20 = (bf16[64,16,128]{2,1,0:T(8,128)(2,1)}, bf16[64,16,128]{2,1,0:T(8,128)(2,1)S(1)}, u32[]{:S(2)}, u32[]{:S(2)}) collective-permute-start(bf16[64,16,128]{2,1,0:T(8,128)(2,1)} %get-tuple-element.119), channel_id=1, source_target_pairs={{0,8},{4,12},{8,0},{12,4},{1,9},{5,13},{9,1},{13,5},{2,10},{6,14},... | collective-permute-start | bytes 786440 | tf_op jit(solution)/shard_map/ppermute | solution.py:596
  330.2 29.2 %collective-permute-start.21 = (bf16[64,16,128]{2,1,0:T(8,128)(2,1)}, bf16[64,16,128]{2,1,0:T(8,128)(2,1)S(1)}, u32[]{:S(2)}, u32[]{:S(2)}) collective-permute-start(bf16[64,16,128]{2,1,0:T(8,128)(2,1)} %get-tuple-element.120), channel_id=1, source_target_pairs={{0,12},{4,0},{8,4},{12,8},{1,13},{5,1},{9,5},{13,9},{2,14},{6,2},{... | collective-permute-start | bytes 786440 | tf_op jit(solution)/shard_map/ppermute | solution.py:596
  (27 other events, 112.0 us)
